TPU v7x, 32 devices: a whole 2x2x4 slice. The times are simulated.
32 devices in a mesh: blk: 8 (over y, x, core), head: 4 (over z).
Axes of the slice: x: 2, y: 2, z: 4, core: 2. Of those that a mesh axis runs over, the one named last changes fastest.
Arguments:
- tokens: bfloat16 [4096, 2048], P(('blk', 'head')), may hold values from -6 to 6
- lengths: int32 [2], replicated, may hold values from 1024 to 2560, as said below
- block_order: int32 [32], replicated, may hold values from 0 to 31, each once
- bucket_of: int32 [257], replicated, may hold values from 0 to 31, as said below
- gain_attn: float32 [2048], P(('blk', 'head')), may hold values from 0.5 to 1.5
- w_query: bfloat16 [2048, 2048], P('blk', 'head'), may hold values from -0.015625 to 0.015625
- w_key: bfloat16 [2048, 2048], P('blk', 'head'), may hold values from -0.125 to 0.125
- w_value: bfloat16 [2048, 2048], P('blk', 'head'), may hold values from -0.125 to 0.125
- w_out: bfloat16 [2048, 2048], P('head', 'blk'), may hold values from -1.5 to 1.5
- bias_table: bfloat16 [32, 32], P('blk', 'head'), may hold values from -4 to 4
- gain_ffn: float32 [2048], P(('blk', 'head')), may hold values from 0.5 to 1.5
- w_gate: bfloat16 [2048, 5120], P('blk', 'head'), may hold values from -0.125 to 0.125
- w_up: bfloat16 [2048, 5120], P('blk', 'head'), may hold values from -0.125 to 0.125
- w_down: bfloat16 [5120, 2048], P('head', 'blk'), may hold values from -0.078125 to 0.078125
- cotangent: bfloat16 [4096, 2048], P(('blk', 'head')), may hold values from -6 to 6
Outputs:
- output: float32 [4096, 2048], P(('blk', 'head'))
- input_grad: float32 [4096, 2048], P(('blk', 'head'))
- grad_gain_attn: float32 [2048], P(('blk', 'head'))
- grad_w_query: float32 [2048, 2048], P('blk', 'head')
- grad_w_key: float32 [2048, 2048], P('blk', 'head')
- grad_w_value: float32 [2048, 2048], P('blk', 'head')
- grad_w_out: float32 [2048, 2048], P('head', 'blk')
- grad_bias_table: float32 [32, 32], P('blk', 'head')
- grad_gain_ffn: float32 [2048], P(('blk', 'head'))
- grad_w_gate: float32 [2048, 5120], P('blk', 'head')
- grad_w_up: float32 [2048, 5120], P('blk', 'head')
- grad_w_down: float32 [5120, 2048], P('head', 'blk')
Inputs may be any that keep to these rules, and one draw needn't show every extreme that they name: lengths[n] is the length of sequence n in the packed order; they add up to 4096, and one of them has exactly 2560 tokens. Rows 128 * i to 128 * i + 127 of tokens and cotangent are the places 128 * block_order[i] onward of the packed order; every block appears once. bucket_of[r + 128] is the bucket of the relative position r (key's place minus query's) for -128 <= r <= 128; farther ones take the bucket of the nearer end. For r <= 0 it lies below 16, for r > 0 at or above; for |r| < 8 it is |r|, plus 32 // 2 when r > 0; it never falls as |r| grows on either side.
All inputs are finite; a program needn't handle non-finite values.
Results may differ from a plain program's by a relative error of at most 0.024.
Values may be sent and summed in bfloat16 or wider, within the bound.
No kernel may reach another device: no remote copies, remote signals or barrier semaphores. Data moves between devices by JAX's collectives and lax.ppermute only.
A program may use at most 192 MiB of HBM per device.

v0:
```python
import jax
import jax.numpy as jnp
from jax import lax
from jax.sharding import PartitionSpec as P

HD = 64
MAXDIST = 128
SPAN = 128


norm_eps = 1e-06
masked_score = -1e30


def shifted(shard, axis, by):
    length = lax.axis_size(axis)
    return lax.ppermute(shard, axis, [(i, (i + by) % length) for i in range(length)])


def gelu_tanh(values):
    return jax.nn.gelu(values, approximate=True)


def rms_scale(values):
    return lax.rsqrt(jnp.mean(values * values, axis=-1, keepdims=True) + norm_eps)


def norm_back(d_normed, source, inv_rms, gain_vec):
    scaled = d_normed * gain_vec
    x_hat = source * inv_rms
    gain_part = jnp.sum(d_normed * x_hat, axis=0)
    d_source = inv_rms * (scaled - x_hat * jnp.mean(scaled * x_hat, axis=-1, keepdims=True))
    return (d_source, gain_part)


def segment_of(places, seq_ends):
    return jnp.sum((places[:, None] >= seq_ends[None, :]).astype(jnp.int32), axis=1)


def product(left_side, right_side):
    return jnp.dot(left_side, right_side, preferred_element_type=jnp.float32)


def rows_inner(left_side, right_side):
    return lax.dot_general(
        left_side, right_side, (((0,), (0,)), ((), ())), preferred_element_type=jnp.float32
    )


def cols_inner(left_side, right_side):
    return lax.dot_general(
        left_side, right_side, (((1,), (1,)), ((), ())), preferred_element_type=jnp.float32
    )


def gather_rows(values):
    return lax.all_gather(values, "head", axis=0, tiled=True)


def sum_rows(partial_rows):
    return lax.psum_scatter(
        partial_rows.astype(jnp.bfloat16), "head", scatter_dimension=0, tiled=True
    ).astype(jnp.float32)


def pass_grads(key_grad, value_grad):
    return (
        shifted(key_grad.astype(jnp.bfloat16), "blk", 1).astype(key_grad.dtype),
        shifted(value_grad.astype(jnp.bfloat16), "blk", 1).astype(value_grad.dtype),
    )


def on_device(
    tokens,
    lengths,
    block_order,
    bucket_of,
    gain_attn,
    w_query,
    w_key,
    w_value,
    w_out,
    bias_table,
    gain_ffn,
    w_gate,
    w_up,
    w_down,
    cotangent,
):
    blk_count = lax.axis_size("blk")
    blk_spot = lax.axis_index("blk")
    block_rows = tokens.shape[0] * lax.axis_size("head")
    width_here = w_query.shape[1]
    heads_here = width_here // HD
    sub_count = block_rows // SPAN
    rel_count = bucket_of.shape[0]
    gain_one, gain_two = (
        lax.all_gather(gain_attn, ("blk", "head"), axis=0, tiled=True),
        lax.all_gather(gain_ffn, ("blk", "head"), axis=0, tiled=True),
    )
    full_query, full_key, full_value, full_out, full_table, full_gate, full_up, full_down = (
        lax.all_gather(w_query, "blk", axis=0, tiled=True),
        lax.all_gather(w_key, "blk", axis=0, tiled=True),
        lax.all_gather(w_value, "blk", axis=0, tiled=True),
        lax.all_gather(w_out, "blk", axis=1, tiled=True),
        lax.all_gather(bias_table, "blk", axis=0, tiled=True),
        lax.all_gather(w_gate, "blk", axis=0, tiled=True),
        lax.all_gather(w_up, "blk", axis=0, tiled=True),
        lax.all_gather(w_down, "blk", axis=1, tiled=True),
    )
    seq_ends = jnp.cumsum(lengths)
    offsets = jnp.arange(SPAN, dtype=jnp.int32)

    def block_ids(anchor):
        return lax.dynamic_slice_in_dim(block_order, anchor * sub_count, sub_count, 0)

    query_ids = block_ids(blk_spot)
    query_seg = segment_of((query_ids[:, None] * SPAN + offsets[None, :]).reshape(-1), seq_ends)
    buckets = (
        bucket_of[:, None] == jnp.arange(full_table.shape[0], dtype=jnp.int32)[None, :]
    ).astype(jnp.float32)
    rel_bias = jnp.dot(buckets, full_table.astype(jnp.float32), precision=lax.Precision.HIGHEST).T
    reach = (MAXDIST + SPAN - 1) // SPAN
    tile_count = 2 * reach + 3
    tile_ids = jnp.arange(tile_count, dtype=jnp.int32)
    tile_step = (tile_ids - (reach + 1)) * SPAN
    rel_near = (
        jnp.clip(
            tile_step[:, None, None] + offsets[None, None, :] - offsets[None, :, None],
            -MAXDIST,
            MAXDIST,
        )
        + MAXDIST
    )
    near_tiles = jnp.take(rel_bias, rel_near, axis=1)
    tokens_wide = tokens.astype(jnp.float32)
    rstd_one = rms_scale(tokens_wide)
    normed_one = (tokens_wide * rstd_one * gain_one).astype(jnp.bfloat16)
    rows_one = gather_rows(normed_one)
    query = product(rows_one, full_query).astype(jnp.bfloat16)
    key_rows = product(rows_one, full_key).astype(jnp.bfloat16)
    value_rows = product(rows_one, full_value).astype(jnp.bfloat16)
    query_heads = query.reshape(block_rows, heads_here, HD)

    def scores_of(q_heads, q_ids, q_seg, key_part, key_id):
        raw_scores = jnp.einsum(
            "qhd,khd->hqk", q_heads, key_part, preferred_element_type=jnp.float32
        )
        key_seg = segment_of(key_id * SPAN + offsets, seq_ends)
        same_seq = q_seg[:, None] == key_seg[None, :]
        step_of = jnp.clip(key_id - q_ids, -(reach + 1), reach + 1) + reach + 1
        picker = (step_of[:, None] == tile_ids[None, :]).astype(jnp.float32)
        bias_part = jnp.einsum("at,htqk->haqk", picker, near_tiles, precision=lax.Precision.HIGHEST)
        return (raw_scores + bias_part.reshape(heads_here, block_rows, SPAN), same_seq, picker)

    def split_block(key_blk, value_blk, anchor):
        return (
            key_blk.reshape(sub_count, SPAN, heads_here, HD),
            value_blk.reshape(sub_count, SPAN, heads_here, HD),
            block_ids(anchor),
        )

    def forward_part(carried, sub_part):
        running_max, running_sum, mix_acc = carried
        key_part, value_part, key_id = sub_part
        scores, same_seq, picker = scores_of(query_heads, query_ids, query_seg, key_part, key_id)
        new_max = jnp.maximum(
            running_max, jnp.max(jnp.where(same_seq[None], scores, masked_score), axis=2)
        )
        weights = jnp.where(same_seq[None], jnp.exp(scores - new_max[:, :, None]), 0.0)
        rescale = jnp.exp(running_max - new_max)
        running_sum = running_sum * rescale + jnp.sum(weights, axis=2)
        mix_acc = mix_acc * rescale[:, :, None] + jnp.einsum(
            "hqk,khd->hqd",
            weights.astype(jnp.bfloat16),
            value_part,
            preferred_element_type=jnp.float32,
        )
        return ((new_max, running_sum, mix_acc), None)

    def forward_block(carried, key_blk, value_blk, anchor):
        carried, unused = lax.scan(forward_part, carried, split_block(key_blk, value_blk, anchor))
        return carried

    start_state = (
        jnp.full((heads_here, block_rows), masked_score, jnp.float32),
        jnp.zeros((heads_here, block_rows), jnp.float32),
        jnp.zeros((heads_here, block_rows, HD), jnp.float32),
    )
    first_state = forward_block(start_state, key_rows, value_rows, blk_spot)

    def forward_turn(turn_num, carried):
        key_blk, value_blk, softmax_state = carried
        key_blk, value_blk = shifted((key_blk, value_blk), "blk", 1)
        anchor = (blk_spot - turn_num) % blk_count
        return (key_blk, value_blk, forward_block(softmax_state, key_blk, value_blk, anchor))

    unused_key, unused_value, (running_max, running_sum, mix_acc) = lax.fori_loop(
        1, blk_count, forward_turn, (key_rows, value_rows, first_state)
    )
    attn_exact = mix_acc / running_sum[:, :, None]
    log_total = running_max + jnp.log(running_sum)
    attn_mix = attn_exact.transpose(1, 0, 2).reshape(block_rows, width_here).astype(jnp.bfloat16)
    hidden_one = tokens_wide + sum_rows(product(attn_mix, full_out))
    rstd_two = rms_scale(hidden_one)
    normed_two = (hidden_one * rstd_two * gain_two).astype(jnp.bfloat16)
    rows_two = gather_rows(normed_two)
    gate_pre = product(rows_two, full_gate)
    up_pre = product(rows_two, full_up)
    activated = (gelu_tanh(gate_pre) * up_pre).astype(jnp.bfloat16)
    output = hidden_one + sum_rows(product(activated, full_down))
    full_query, full_key, full_value, full_out, full_gate, full_up, full_down = (
        lax.all_gather(w_query, "blk", axis=0, tiled=True),
        lax.all_gather(w_key, "blk", axis=0, tiled=True),
        lax.all_gather(w_value, "blk", axis=0, tiled=True),
        lax.all_gather(w_out, "blk", axis=1, tiled=True),
        lax.all_gather(w_gate, "blk", axis=0, tiled=True),
        lax.all_gather(w_up, "blk", axis=0, tiled=True),
        lax.all_gather(w_down, "blk", axis=1, tiled=True),
    )
    rows_one, rows_two = (
        lax.all_gather(normed_one, "head", axis=0, tiled=True),
        lax.all_gather(normed_two, "head", axis=0, tiled=True),
    )
    gate_pre = product(rows_two, full_gate)
    up_pre = product(rows_two, full_up)
    activated = (gelu_tanh(gate_pre) * up_pre).astype(jnp.bfloat16)
    rows_grad = gather_rows(cotangent)
    grad_down = rows_inner(activated, rows_grad)
    d_hidden = cols_inner(rows_grad, full_down)
    gelu_vals, gelu_pull = jax.vjp(gelu_tanh, gate_pre)
    d_upper = (d_hidden * gelu_vals).astype(jnp.bfloat16)
    d_gate = gelu_pull(d_hidden * up_pre)[0].astype(jnp.bfloat16)
    grad_gate = rows_inner(rows_two, d_gate)
    grad_up = rows_inner(rows_two, d_upper)
    d_normed_two = sum_rows(cols_inner(d_gate, full_gate) + cols_inner(d_upper, full_up))
    d_source_two, gain_part_two = norm_back(d_normed_two, hidden_one, rstd_two, gain_two)
    d_hidden_one = cotangent.astype(jnp.float32) + d_source_two
    rows_attn = gather_rows(d_hidden_one.astype(jnp.bfloat16))
    grad_out = rows_inner(attn_mix, rows_attn)
    d_mix = cols_inner(rows_attn, full_out).astype(jnp.bfloat16)
    d_mix_heads = d_mix.reshape(block_rows, heads_here, HD)
    row_delta = jnp.sum(d_mix_heads.astype(jnp.float32).transpose(1, 0, 2) * attn_exact, axis=-1)

    def back_tile(q_heads, q_ids, q_seg, mix_grad, totals, deltas, key_part, value_part, key_id):
        scores, same_seq, picker = scores_of(q_heads, q_ids, q_seg, key_part, key_id)
        weights_back = jnp.where(same_seq[None], jnp.exp(scores - totals[:, :, None]), 0.0)
        d_probs = jnp.einsum(
            "qhd,khd->hqk", mix_grad, value_part, preferred_element_type=jnp.float32
        )
        d_scores = (weights_back * (d_probs - deltas[:, :, None])).astype(jnp.bfloat16)
        d_query_part = jnp.einsum(
            "hqk,khd->qhd", d_scores, key_part, preferred_element_type=jnp.float32
        )
        d_key_part = jnp.einsum(
            "hqk,qhd->khd", d_scores, q_heads, preferred_element_type=jnp.float32
        )
        d_value_part = jnp.einsum(
            "hqk,qhd->khd",
            weights_back.astype(jnp.bfloat16),
            mix_grad,
            preferred_element_type=jnp.float32,
        )
        d_near_part = jnp.einsum(
            "at,haqk->htqk",
            picker,
            d_scores.astype(jnp.float32).reshape(heads_here, sub_count, SPAN, SPAN),
            precision=lax.Precision.HIGHEST,
        )
        return (d_query_part, d_key_part, d_value_part, d_near_part)

    zero_grads = jnp.zeros((block_rows, width_here), jnp.float32)
    zero_query = jnp.zeros((block_rows, heads_here, HD), jnp.float32)
    zero_near = jnp.zeros(near_tiles.shape, jnp.float32)

    def backward_part(carried, sub_part):
        d_query, d_near = carried
        key_part, value_part, key_id = sub_part
        dq_part, dk_part, dv_part, dn_part = back_tile(
            query_heads,
            query_ids,
            query_seg,
            d_mix_heads,
            log_total,
            row_delta,
            key_part,
            value_part,
            key_id,
        )
        return ((d_query + dq_part, d_near + dn_part), (dk_part, dv_part))

    def backward_block(carried, key_blk, value_blk, anchor, key_grad, value_grad):
        carried, (key_parts, value_parts) = lax.scan(
            backward_part, carried, split_block(key_blk, value_blk, anchor)
        )
        key_grad = key_grad + key_parts.reshape(block_rows, width_here)
        value_grad = value_grad + value_parts.reshape(block_rows, width_here)
        return (carried, key_grad, value_grad)

    back_state, key_grad, value_grad = backward_block(
        (zero_query, zero_near), key_rows, value_rows, blk_spot, zero_grads, zero_grads
    )

    def backward_turn(turn_num, carried):
        key_blk, value_blk, inner_state, key_grad, value_grad = carried
        key_blk, value_blk = shifted((key_blk, value_blk), "blk", 1)
        key_grad, value_grad = pass_grads(key_grad, value_grad)
        anchor = (blk_spot - turn_num) % blk_count
        inner_state, key_grad, value_grad = backward_block(
            inner_state, key_blk, value_blk, anchor, key_grad, value_grad
        )
        return (key_blk, value_blk, inner_state, key_grad, value_grad)

    unused_key, unused_value, (d_query, d_near), key_grad, value_grad = lax.fori_loop(
        1, blk_count, backward_turn, (key_rows, value_rows, back_state, key_grad, value_grad)
    )
    key_grad, value_grad = pass_grads(key_grad, value_grad)
    flat_near = rel_near.reshape(-1)
    d_rel = jax.vmap(
        lambda row_vals: jax.ops.segment_sum(row_vals, flat_near, num_segments=rel_count)
    )(d_near.reshape(heads_here, -1))
    d_query_low = d_query.reshape(block_rows, width_here).astype(jnp.bfloat16)
    d_key_low = key_grad.astype(jnp.bfloat16)
    d_value_low = value_grad.astype(jnp.bfloat16)
    grad_query = rows_inner(rows_one, d_query_low)
    grad_key = rows_inner(rows_one, d_key_low)
    grad_value = rows_inner(rows_one, d_value_low)
    grad_table = jnp.dot(buckets.T, d_rel.T, precision=lax.Precision.HIGHEST)
    d_normed_one = sum_rows(
        cols_inner(d_query_low, full_query)
        + cols_inner(d_key_low, full_key)
        + cols_inner(d_value_low, full_value)
    )
    d_source_one, gain_part_one = norm_back(d_normed_one, tokens_wide, rstd_one, gain_one)
    input_grad = d_hidden_one + d_source_one
    reduced = (
        lax.psum_scatter(
            grad_query.astype(jnp.bfloat16), "blk", scatter_dimension=0, tiled=True
        ).astype(jnp.float32),
        lax.psum_scatter(
            grad_key.astype(jnp.bfloat16), "blk", scatter_dimension=0, tiled=True
        ).astype(jnp.float32),
        lax.psum_scatter(
            grad_value.astype(jnp.bfloat16), "blk", scatter_dimension=0, tiled=True
        ).astype(jnp.float32),
        lax.psum_scatter(
            grad_out.astype(jnp.bfloat16), "blk", scatter_dimension=1, tiled=True
        ).astype(jnp.float32),
        lax.psum_scatter(
            grad_table.astype(jnp.bfloat16), "blk", scatter_dimension=0, tiled=True
        ).astype(jnp.float32),
        lax.psum_scatter(
            grad_gate.astype(jnp.bfloat16), "blk", scatter_dimension=0, tiled=True
        ).astype(jnp.float32),
        lax.psum_scatter(
            grad_up.astype(jnp.bfloat16), "blk", scatter_dimension=0, tiled=True
        ).astype(jnp.float32),
        lax.psum_scatter(
            grad_down.astype(jnp.bfloat16), "blk", scatter_dimension=1, tiled=True
        ).astype(jnp.float32),
    )
    gain_sums = (
        lax.psum_scatter(gain_part_one, ("blk", "head"), scatter_dimension=0, tiled=True),
        lax.psum_scatter(gain_part_two, ("blk", "head"), scatter_dimension=0, tiled=True),
    )
    return (
        output,
        input_grad,
        gain_sums[0],
        reduced[0],
        reduced[1],
        reduced[2],
        reduced[3],
        reduced[4],
        gain_sums[1],
        reduced[5],
        reduced[6],
        reduced[7],
    )


def solution(mesh):
    in_specs = (
        P(("blk", "head"), None),
        P(),
        P(),
        P(),
        P(("blk", "head")),
        P("blk", "head"),
        P("blk", "head"),
        P("blk", "head"),
        P("head", "blk"),
        P("blk", "head"),
        P(("blk", "head")),
        P("blk", "head"),
        P("blk", "head"),
        P("head", "blk"),
        P(("blk", "head"), None),
    )
    out_specs = (
        P(("blk", "head"), None),
        P(("blk", "head"), None),
        P(("blk", "head")),
        P("blk", "head"),
        P("blk", "head"),
        P("blk", "head"),
        P("head", "blk"),
        P("blk", "head"),
        P(("blk", "head")),
        P("blk", "head"),
        P("blk", "head"),
        P("head", "blk"),
    )
    return jax.shard_map(
        on_device, mesh=mesh, in_specs=in_specs, out_specs=out_specs, check_vma=False
    )
```

profile of v0, /device:TPU:0, one launch (start us, length us, event | category | flops | bytes accessed | tf_op | source)
XLA Modules:
  0.0 3777.2 jit_solution(8224683241666510555)
XLA Ops:
  10.3 42.0 %all-reduce.6 = (f32[2048]{0:T(1024)S(1)}, f32[2048]{0:T(1024)}) all-reduce(f32[2048]{0:T(1024)S(1)} %dynamic-update-slice, f32[2048]{0:T(1024)S(1)} %dynamic-update-slice.1), channel_id=1, replica_groups=mesh['blk'=8,'head'=4] {'blk','head'}, use_global_device_ids=true, to_apply=%add | all-reduce | flops 4096 | bytes 32768
  68.6 271.2 %gather_fusion = f32[81920,8]{1,0:T(8,128)} fusion(f32[8,257]{0,1:T(8,128)S(1)} %copy.149, s32[81920]{0:T(1024)S(1)} %broadcast_clamp_fusion), kind=kCustom, calls=%fused_computation | custom fusion | bytes 5570560 | tf_op jit(solution)/shard_map/jit(_take)/gather | solution.py:135
  387.5 84.4 %while.176 = (s32[]{:T(128)}, f32[8,512]{1,0:T(8,128)S(1)}, f32[8,512]{1,0:T(8,128)S(1)}, f32[8,512,64]{1,2,0:T(8,128)S(1)}, s32[512]{0:T(512)S(1)}, /*index=5*/...) while((s32[]{:T(128)}, f32[8,512]{1,0:T(8,128)S(1)}, ...), condition=%wide.region_7.8_spmd.clone, body=%wide.region_3.7_spmd.clone.sunk | while | flops 171266848 | bytes 33296656 | solution.py:182
  472.8 569.8 %while.173 = (s32[]{:T(128)}, bf16[512,512]{0,1:T(8,128)(2,1)}, bf16[512,512]{0,1:T(8,128)(2,1)}, f32[8,512]{1,0:T(8,128)S(1)}, f32[8,512]{1,0:T(8,128)S(1)}, /*...) while((s32[]{:T(128)}, bf16[512,512]{0,1:T(8,128)(2,1)}, ...), condition=%wide.region_14.15_spmd.clone, body=%wide.region_8.14_spmd.clone.sunk | while | flops 170992432 | bytes 48240740 | solution.py:198
  491.9 58.7 %while.178 = (s32[]{:T(128)}, f32[8,512]{1,0:T(8,128)S(1)}, f32[8,512]{1,0:T(8,128)}, f32[8,512,64]{1,2,0:T(8,128)S(1)}, s32[512]{0:T(512)S(1)}, /*index=5*/s32[...) while((s32[]{:T(128)}, f32[8,512]{1,0:T(8,128)S(1)}, ...), condition=%wide.region_13.13_spmd, body=%wide.region_9.12_spmd.sunk | while | flops 170992416 | bytes 33428352 | solution.py:182
  573.3 58.7 %while.178 = (s32[]{:T(128)}, f32[8,512]{1,0:T(8,128)S(1)}, f32[8,512]{1,0:T(8,128)}, f32[8,512,64]{1,2,0:T(8,128)S(1)}, s32[512]{0:T(512)S(1)}, /*index=5*/s32[...) while((s32[]{:T(128)}, f32[8,512]{1,0:T(8,128)S(1)}, ...), condition=%wide.region_13.13_spmd, body=%wide.region_9.12_spmd.sunk | while | flops 170992416 | bytes 33428352 | solution.py:182
  654.7 58.7 %while.178 = (s32[]{:T(128)}, f32[8,512]{1,0:T(8,128)S(1)}, f32[8,512]{1,0:T(8,128)}, f32[8,512,64]{1,2,0:T(8,128)S(1)}, s32[512]{0:T(512)S(1)}, /*index=5*/s32[...) while((s32[]{:T(128)}, f32[8,512]{1,0:T(8,128)S(1)}, ...), condition=%wide.region_13.13_spmd, body=%wide.region_9.12_spmd.sunk | while | flops 170992416 | bytes 33428352 | solution.py:182
  736.1 58.7 %while.178 = (s32[]{:T(128)}, f32[8,512]{1,0:T(8,128)S(1)}, f32[8,512]{1,0:T(8,128)}, f32[8,512,64]{1,2,0:T(8,128)S(1)}, s32[512]{0:T(512)S(1)}, /*index=5*/s32[...) while((s32[]{:T(128)}, f32[8,512]{1,0:T(8,128)S(1)}, ...), condition=%wide.region_13.13_spmd, body=%wide.region_9.12_spmd.sunk | while | flops 170992416 | bytes 33428352 | solution.py:182
  817.4 58.7 %while.178 = (s32[]{:T(128)}, f32[8,512]{1,0:T(8,128)S(1)}, f32[8,512]{1,0:T(8,128)}, f32[8,512,64]{1,2,0:T(8,128)S(1)}, s32[512]{0:T(512)S(1)}, /*index=5*/s32[...) while((s32[]{:T(128)}, f32[8,512]{1,0:T(8,128)S(1)}, ...), condition=%wide.region_13.13_spmd, body=%wide.region_9.12_spmd.sunk | while | flops 170992416 | bytes 33428352 | solution.py:182
  898.8 58.7 %while.178 = (s32[]{:T(128)}, f32[8,512]{1,0:T(8,128)S(1)}, f32[8,512]{1,0:T(8,128)}, f32[8,512,64]{1,2,0:T(8,128)S(1)}, s32[512]{0:T(512)S(1)}, /*index=5*/s32[...) while((s32[]{:T(128)}, f32[8,512]{1,0:T(8,128)S(1)}, ...), condition=%wide.region_13.13_spmd, body=%wide.region_9.12_spmd.sunk | while | flops 170992416 | bytes 33428352 | solution.py:182
  980.2 58.7 %while.178 = (s32[]{:T(128)}, f32[8,512]{1,0:T(8,128)S(1)}, f32[8,512]{1,0:T(8,128)}, f32[8,512,64]{1,2,0:T(8,128)S(1)}, s32[512]{0:T(512)S(1)}, /*index=5*/s32[...) while((s32[]{:T(128)}, f32[8,512]{1,0:T(8,128)S(1)}, ...), condition=%wide.region_13.13_spmd, body=%wide.region_9.12_spmd.sunk | while | flops 170992416 | bytes 33428352 | solution.py:182
  1132.6 48.2 %all-gather.23.cloned.1.call-done = bf16[512,2048]{1,0:T(8,128)(2,1)} async-done(((bf16[128,2048]{1,0:T(8,128)(2,1)}), bf16[512,2048]{1,0:T(8,128)(2,1)}) %all-gather.23.cloned.1.call-update) | async-done | bytes 2097168 | tf_op jit(solution)/shard_map/all_gather | solution.py:57
  1270.2 42.8 %all-gather.29.cloned.1.call-done = bf16[1280,2048]{1,0:T(8,128)(2,1)} async-done(((bf16[1280,256]{1,0:T(8,128)(2,1)}), bf16[1280,2048]{1,0:T(8,128)(2,1)}) %all-gather.29.cloned.1.call-update) | async-done | bytes 5242896 | tf_op jit(solution)/shard_map/all_gather | solution.py:109
  1333.5 44.0 %reduce-scatter.16.cloned.1.call-done = bf16[128,2048]{1,0:T(8,128)(2,1)} async-done(((bf16[512,2048]{1,0:T(8,128)(2,1)}), bf16[128,2048]{1,0:T(8,128)(2,1)}) %reduce-scatter.16.cloned.1.call-update) | async-done | bytes 524304 | tf_op jit(solution)/shard_map/reduce_scatter | solution.py:61
  1433.2 187.5 %while.177 = (s32[]{:T(128)}, f32[512,8,64]{0,2,1:T(8,128)}, f32[8,5,128,128]{3,1,2,0:T(8,128)}, bf16[4,128,8,64]{1,0,3,2:T(4,128)(2,1)}, bf16[4,128,8,64]{1,0,3...) while((s32[]{:T(128)}, f32[512,8,64]{0,2,1:T(8,128)}, ...), condition=%wide.region_23.24_spmd.clone, body=%wide.region_21.23_spmd.clone.sunk | while | flops 377815872 | bytes 45650252 | solution.py:293
  1623.1 1484.5 %while.175 = (s32[]{:T(128)}, bf16[512,512]{0,1:T(8,128)(2,1)S(1)}, bf16[512,512]{0,1:T(8,128)(2,1)S(1)}, f32[512,8,64]{0,2,1:T(8,128)}, f32[8,5,128,128]{3,1,2,...) while((s32[]{:T(128)}, bf16[512,512]{0,1:T(8,128)(2,1)S(1)}, ...), condition=%wide.region_28.29_spmd.clone, body=%wide.region_24.28_spmd.clone.sunk | while | flops 378471264 | bytes 77109544 | solution.py:314
  1639.5 189.5 %while.179 = (s32[]{:T(128)}, f32[512,8,64]{0,2,1:T(8,128)}, f32[8,5,128,128]{3,1,2,0:T(8,128)}, f32[4,128,8,64]{1,0,3,2:T(4,128)}, f32[4,128,8,64]{1,0,3,2:T(4,...) while((s32[]{:T(128)}, f32[512,8,64]{0,2,1:T(8,128)}, ...), condition=%wide.region_27.27_spmd, body=%wide.region_25.26_spmd.sunk | while | flops 376898368 | bytes 45650848 | solution.py:293
  1851.6 189.5 %while.179 = (s32[]{:T(128)}, f32[512,8,64]{0,2,1:T(8,128)}, f32[8,5,128,128]{3,1,2,0:T(8,128)}, f32[4,128,8,64]{1,0,3,2:T(4,128)}, f32[4,128,8,64]{1,0,3,2:T(4,...) while((s32[]{:T(128)}, f32[512,8,64]{0,2,1:T(8,128)}, ...), condition=%wide.region_27.27_spmd, body=%wide.region_25.26_spmd.sunk | while | flops 376898368 | bytes 45650848 | solution.py:293
  2063.6 189.5 %while.179 = (s32[]{:T(128)}, f32[512,8,64]{0,2,1:T(8,128)}, f32[8,5,128,128]{3,1,2,0:T(8,128)}, f32[4,128,8,64]{1,0,3,2:T(4,128)}, f32[4,128,8,64]{1,0,3,2:T(4,...) while((s32[]{:T(128)}, f32[512,8,64]{0,2,1:T(8,128)}, ...), condition=%wide.region_27.27_spmd, body=%wide.region_25.26_spmd.sunk | while | flops 376898368 | bytes 45650848 | solution.py:293
  2275.6 189.5 %while.179 = (s32[]{:T(128)}, f32[512,8,64]{0,2,1:T(8,128)}, f32[8,5,128,128]{3,1,2,0:T(8,128)}, f32[4,128,8,64]{1,0,3,2:T(4,128)}, f32[4,128,8,64]{1,0,3,2:T(4,...) while((s32[]{:T(128)}, f32[512,8,64]{0,2,1:T(8,128)}, ...), condition=%wide.region_27.27_spmd, body=%wide.region_25.26_spmd.sunk | while | flops 376898368 | bytes 45650848 | solution.py:293
  2487.6 189.5 %while.179 = (s32[]{:T(128)}, f32[512,8,64]{0,2,1:T(8,128)}, f32[8,5,128,128]{3,1,2,0:T(8,128)}, f32[4,128,8,64]{1,0,3,2:T(4,128)}, f32[4,128,8,64]{1,0,3,2:T(4,...) while((s32[]{:T(128)}, f32[512,8,64]{0,2,1:T(8,128)}, ...), condition=%wide.region_27.27_spmd, body=%wide.region_25.26_spmd.sunk | while | flops 376898368 | bytes 45650848 | solution.py:293
  2699.7 189.5 %while.179 = (s32[]{:T(128)}, f32[512,8,64]{0,2,1:T(8,128)}, f32[8,5,128,128]{3,1,2,0:T(8,128)}, f32[4,128,8,64]{1,0,3,2:T(4,128)}, f32[4,128,8,64]{1,0,3,2:T(4,...) while((s32[]{:T(128)}, f32[512,8,64]{0,2,1:T(8,128)}, ...), condition=%wide.region_27.27_spmd, body=%wide.region_25.26_spmd.sunk | while | flops 376898368 | bytes 45650848 | solution.py:293
  2911.7 189.5 %while.179 = (s32[]{:T(128)}, f32[512,8,64]{0,2,1:T(8,128)}, f32[8,5,128,128]{3,1,2,0:T(8,128)}, f32[4,128,8,64]{1,0,3,2:T(4,128)}, f32[4,128,8,64]{1,0,3,2:T(4,...) while((s32[]{:T(128)}, f32[512,8,64]{0,2,1:T(8,128)}, ...), condition=%wide.region_27.27_spmd, body=%wide.region_25.26_spmd.sunk | while | flops 376898368 | bytes 45650848 | solution.py:293
  3192.1 506.6 %scatter_custom_fusion = f32[8,257]{0,1:T(8,128)S(1)} fusion(s32[81920]{0:T(1024)S(1)} %bitcast.408, f32[81920,8]{1,0:T(8,128)} %copy.163, f32[]{:T(128)} %constant.391.clone.1), kind=kCustom, calls=%fused_computation.205 | custom fusion | flops 655360 | bytes 8736 | tf_op jit(solution)/shard_map/vmap()/scatter-add | solution.py:320
  (1975 shorter events, 2757.4 us)
Async XLA Ops:
  7.2 363.5 %all-gather.13.cloned.1.call-start = ((), (), s32[]{:S(2)}) async-start(), calls=%async_computation.11 | async-start | bytes 2621440 | tf_op jit(solution)/shard_map/all_gather | solution.py:57
  54.3 316.3 %all-gather.15.cloned.1.call-start = ((), (), s32[]{:S(2)}) async-start(), calls=%async_computation.12 | async-start | bytes 2359296 | tf_op jit(solution)/shard_map/all_gather | solution.py:103
  55.1 320.3 %all-gather.17.cloned.1.call-start = ((), (), s32[]{:S(2)}) async-start(), calls=%async_computation.13 | async-start | bytes 2359296 | tf_op jit(solution)/shard_map/all_gather | solution.py:104
  55.8 328.1 %all-gather.19.cloned.1.call-start = ((), (), s32[]{:S(2)}) async-start(), calls=%async_computation.14 | async-start | bytes 2359296 | tf_op jit(solution)/shard_map/all_gather | solution.py:102
  56.4 986.5 %all-gather.21.cloned.1.call-start = ((), (), s32[]{:S(2)}) async-start(), calls=%async_computation.15 | async-start | bytes 2359296 | tf_op jit(solution)/shard_map/all_gather | solution.py:105
  57.0 1033.1 %reduce-scatter.12.cloned.1.call-start = ((), (), s32[]{:S(2)}) async-start(), calls=%async_computation.16 | async-start | bytes 2621440 | tf_op jit(solution)/shard_map/reduce_scatter | solution.py:61
  1094.8 218.2 %all-gather.29.cloned.1.call-start = ((), (), s32[]{:S(2)}) async-start(), calls=%async_computation.20 | async-start | bytes 5898240 | tf_op jit(solution)/shard_map/all_gather | solution.py:109
  1095.5 282.0 %reduce-scatter.16.cloned.1.call-start = ((), (), s32[]{:S(2)}) async-start(), calls=%async_computation.23 | async-start | bytes 2621440 | tf_op jit(solution)/shard_map/reduce_scatter | solution.py:61
  1382.2 2329.5 %reduce-scatter.28.cloned.1.call-start = ((), (), s32[]{:S(2)}) async-start(), calls=%async_computation.30 | async-start | bytes 5898240 | tf_op jit(solution)/shard_map/reduce_scatter | solution.py:352
  1389.7 2324.3 %reduce-scatter.30.cloned.1.call-start = ((), (), s32[]{:S(2)}) async-start(), calls=%async_computation.31 | async-start | bytes 5898240 | tf_op jit(solution)/shard_map/reduce_scatter | solution.py:355
  1397.0 2319.2 %reduce-scatter.32.cloned.1.call-start = ((), (), s32[]{:S(2)}) async-start(), calls=%async_computation.32 | async-start | bytes 5898240 | tf_op jit(solution)/shard_map/reduce_scatter | solution.py:358
  1404.9 2313.6 %reduce-scatter.20.cloned.1.call-start = ((), (), s32[]{:S(2)}) async-start(), calls=%async_computation.26 | async-start | bytes 2359296 | tf_op jit(solution)/shard_map/reduce_scatter | solution.py:337
  1836.5 208.8 %collective-permute-start.3 = (bf16[512,512]{0,1:T(8,128)(2,1)}, bf16[512,512]{0,1:T(8,128)(2,1)}, u32[]{:S(2)}, u32[]{:S(2)}) collective-permute-start(bf16[512,512]{0,1:T(8,128)(2,1)} %get-tuple-element.3382), channel_id=1, source_target_pairs={{0,4},{4,8},{8,12},{12,16},{16,20},{20,24},{24,28},{28,0},{1,5},{5... | collective-permute-start | bytes 1572872 | tf_op jit(solution)/shard_map/while/body/eval_jaxpr/ppermute | solution.py:17
  2047.7 209.7 %collective-permute-start.3 = (bf16[512,512]{0,1:T(8,128)(2,1)}, bf16[512,512]{0,1:T(8,128)(2,1)}, u32[]{:S(2)}, u32[]{:S(2)}) collective-permute-start(bf16[512,512]{0,1:T(8,128)(2,1)} %get-tuple-element.3382), channel_id=1, source_target_pairs={{0,4},{4,8},{8,12},{12,16},{16,20},{20,24},{24,28},{28,0},{1,5},{5... | collective-permute-start | bytes 1572872 | tf_op jit(solution)/shard_map/while/body/eval_jaxpr/ppermute | solution.py:17
  2259.4 207.9 %collective-permute-start.2 = (bf16[512,512]{0,1:T(8,128)(2,1)}, bf16[512,512]{0,1:T(8,128)(2,1)}, u32[]{:S(2)}, u32[]{:S(2)}) collective-permute-start(bf16[512,512]{0,1:T(8,128)(2,1)} %get-tuple-element.3381), channel_id=1, source_target_pairs={{0,4},{4,8},{8,12},{12,16},{16,20},{20,24},{24,28},{28,0},{1,5},{5... | collective-permute-start | bytes 1572872 | tf_op jit(solution)/shard_map/while/body/eval_jaxpr/ppermute | solution.py:17
  2259.7 209.8 %collective-permute-start.3 = (bf16[512,512]{0,1:T(8,128)(2,1)}, bf16[512,512]{0,1:T(8,128)(2,1)}, u32[]{:S(2)}, u32[]{:S(2)}) collective-permute-start(bf16[512,512]{0,1:T(8,128)(2,1)} %get-tuple-element.3382), channel_id=1, source_target_pairs={{0,4},{4,8},{8,12},{12,16},{16,20},{20,24},{24,28},{28,0},{1,5},{5... | collective-permute-start | bytes 1572872 | tf_op jit(solution)/shard_map/while/body/eval_jaxpr/ppermute | solution.py:17
  2471.7 209.8 %collective-permute-start.3 = (bf16[512,512]{0,1:T(8,128)(2,1)}, bf16[512,512]{0,1:T(8,128)(2,1)}, u32[]{:S(2)}, u32[]{:S(2)}) collective-permute-start(bf16[512,512]{0,1:T(8,128)(2,1)} %get-tuple-element.3382), channel_id=1, source_target_pairs={{0,4},{4,8},{8,12},{12,16},{16,20},{20,24},{24,28},{28,0},{1,5},{5... | collective-permute-start | bytes 1572872 | tf_op jit(solution)/shard_map/while/body/eval_jaxpr/ppermute | solution.py:17
  2683.7 209.8 %collective-permute-start.3 = (bf16[512,512]{0,1:T(8,128)(2,1)}, bf16[512,512]{0,1:T(8,128)(2,1)}, u32[]{:S(2)}, u32[]{:S(2)}) collective-permute-start(bf16[512,512]{0,1:T(8,128)(2,1)} %get-tuple-element.3382), channel_id=1, source_target_pairs={{0,4},{4,8},{8,12},{12,16},{16,20},{20,24},{24,28},{28,0},{1,5},{5... | collective-permute-start | bytes 1572872 | tf_op jit(solution)/shard_map/while/body/eval_jaxpr/ppermute | solution.py:17
  2895.7 209.8 %collective-permute-start.3 = (bf16[512,512]{0,1:T(8,128)(2,1)}, bf16[512,512]{0,1:T(8,128)(2,1)}, u32[]{:S(2)}, u32[]{:S(2)}) collective-permute-start(bf16[512,512]{0,1:T(8,128)(2,1)} %get-tuple-element.3382), channel_id=1, source_target_pairs={{0,4},{4,8},{8,12},{12,16},{16,20},{20,24},{24,28},{28,0},{1,5},{5... | collective-permute-start | bytes 1572872 | tf_op jit(solution)/shard_map/while/body/eval_jaxpr/ppermute | solution.py:17
  3113.3 607.2 %reduce-scatter.26.cloned.1.call-start = ((), (), s32[]{:S(2)}) async-start(), calls=%async_computation.29 | async-start | bytes 2359296 | tf_op jit(solution)/shard_map/reduce_scatter | solution.py:346
  3116.9 605.4 %reduce-scatter.22.cloned.1.call-start = ((), (), s32[]{:S(2)}) async-start(), calls=%async_computation.27 | async-start | bytes 2359296 | tf_op jit(solution)/shard_map/reduce_scatter | solution.py:340
  3129.8 594.2 %reduce-scatter.24.cloned.1.call-start = ((), (), s32[]{:S(2)}) async-start(), calls=%async_computation.28 | async-start | bytes 2359296 | tf_op jit(solution)/shard_map/reduce_scatter | solution.py:343
  3149.7 576.2 %reduce-scatter.18.cloned.1.call-start = ((), (), s32[]{:S(2)}) async-start(), calls=%async_computation.25 | async-start | bytes 2621440 | tf_op jit(solution)/shard_map/reduce_scatter | solution.py:61
  3157.1 609.7 %reduce-scatter.14.cloned.1.call-start = ((), (), s32[]{:S(2)}) async-start(), calls=%async_computation.21 | async-start | bytes 2621440 | tf_op jit(solution)/shard_map/reduce_scatter | solution.py:61
  (320 other events, 5281.9 us)
Sparse Core Ops, SparseCore 0:
  54.5 46.4 all-gather.12
  102.8 26.5 all-gather.14
  131.4 27.8 all-gather.16
  161.0 27.8 all-gather.18
  190.7 28.1 all-gather.20
  1048.0 42.0 reduce-scatter.11
  1092.1 40.4 all-gather.24
  1134.9 45.9 all-gather.22
  1182.9 39.8 all-gather.26
  1224.2 45.9 all-gather.30
  1272.2 40.7 all-gather.28
  1333.6 43.8 reduce-scatter.15
  1382.3 45.2 all-gather.32
  1430.8 55.3 reduce-scatter.27
  1489.8 56.5 reduce-scatter.29
  1549.6 56.5 reduce-scatter.31
  3113.4 42.4 reduce-scatter.19
  3159.1 41.2 reduce-scatter.25
  3204.0 41.2 reduce-scatter.21
  3248.4 41.2 reduce-scatter.23
  3292.1 43.7 reduce-scatter.17
  3338.2 43.2 reduce-scatter.13
where the time goes:
time: 3810 us; the launch traced here: 3780 us
  local copies, waits for them, and re-layouts  1460 us (38%)
  matrix products  977 us (26%)
  other arithmetic  648 us (17%)
  waiting for transfers between devices  499 us (13%)
  blocking collectives  103 us (3%)
  loops' own time  49.3 us (1%)
    scatter-add x1, other arithmetic, on_device(): jax.ops.segment_sum(row_vals, flat_near, num_segments=rel_count)  507 us
    dynamic_update_slice x64, local copies, waits for them, and re-layouts, backward_block(): lax.scan(backward_part, carried, split_block(key_blk, value_blk, anchor))  480 us
    dot_general x64, matrix products, scores_of(): jnp.einsum('at,htqk->haqk', picker, near_tiles, precision=lax.Precision.H...  319 us
    gather x2, local copies, waits for them, and re-layouts, on_device(): near_tiles = jnp.take(rel_bias, rel_near, axis=1)  297 us
    transpose x64, local copies, waits for them, and re-layouts, scores_of(): jnp.einsum('at,htqk->haqk', picker, near_tiles, precision=lax.Precision.H...  185 us
    ppermute x44, waiting for transfers between devices, shifted(): lax.ppermute(shard, axis, [(i, (i + by) % length) for i in range(length)])  184 us
    dot_general x32, matrix products, back_tile(): jnp.einsum('at,haqk->htqk', picker, d_scores.astype(jnp.float32).reshape(...  171 us
    reshape x64, local copies, waits for them, and re-layouts, back_tile(): d_scores.astype(jnp.float32).reshape(heads_here, sub_count, SPAN, SPAN)  151 us
  transfers between devices with their start and end apart: 66, of which 38 were waited for; matrix products, arithmetic and copies ran while one was open for 80% of the time, Pallas kernels for 0%

commit v1 on v0

v1 whole, which is shorter than its diff:
```python
import functools

import jax
import jax.numpy as jnp
import numpy as np
from jax import lax
from jax.experimental import pallas as pl
from jax.experimental.pallas import tpu as pltpu
from jax.sharding import PartitionSpec as P

HD = 64
LANES = 2 * HD
MAXDIST = 128
SPAN = 128
BQ = 256
BK = 512
OFF = BK + 2 * SPAN
TABLE_ROWS = 2 * BK + BQ + 4 * SPAN
MID_BLOCKS = BQ // SPAN + 2
WIDE = 2 * BQ
EXTRA = 16
KT_ROWS = 80

norm_eps = 1e-06
masked_score = -1e30
f32 = jnp.float32
bf16 = jnp.bfloat16
MIB = 1 << 20


def rms_scale(values):
    return lax.rsqrt(jnp.mean(values * values, axis=-1, keepdims=True) + norm_eps)


def norm_back(d_normed, source, inv_rms, gain_vec):
    scaled = d_normed * gain_vec
    x_hat = source * inv_rms
    gain_part = jnp.sum(d_normed * x_hat, axis=0)
    d_source = inv_rms * (scaled - x_hat * jnp.mean(scaled * x_hat, axis=-1, keepdims=True))
    return (d_source, gain_part)


def dot_nn(left, right):
    return jnp.dot(left, right, preferred_element_type=f32)


def dot_nt(left, right):
    return lax.dot_general(left, right, (((1,), (1,)), ((), ())), preferred_element_type=f32)


def dot_tn(left, right):
    return lax.dot_general(left, right, (((0,), (0,)), ((), ())), preferred_element_type=f32)


def cyclic(count, by):
    return [(i, (i + by) % count) for i in range(count)]


def gather_slots(rows):
    count = lax.axis_size("head")
    if count != 4:
        return [rows] + [lax.ppermute(rows, "head", cyclic(count, s)) for s in range(1, count)]
    me = lax.axis_index("head")
    back_one = lax.ppermute(rows, "head", cyclic(4, 1))
    ahead_one = lax.ppermute(rows, "head", cyclic(4, 3))
    passed = jnp.where(me == 1, ahead_one, jnp.where(me == 2, back_one, rows))
    back_two = lax.ppermute(passed, "head", [(1, 0), (3, 1), (0, 2), (2, 3)])
    return [rows, back_one, back_two, ahead_one]


def sum_slots(parts):
    count = lax.axis_size("head")
    if count != 4:
        total = parts[0].astype(f32)
        for s in range(1, count):
            total = total + lax.ppermute(parts[s], "head", cyclic(count, count - s)).astype(f32)
        return total
    me = lax.axis_index("head")
    far = lax.ppermute(parts[2], "head", [(0, 1), (1, 3), (2, 0), (3, 2)])
    far_wide = far.astype(f32)
    to_back = jnp.where(me == 2, parts[1].astype(f32) + far_wide, parts[1].astype(f32)).astype(bf16)
    to_ahead = jnp.where(me == 1, parts[3].astype(f32) + far_wide, parts[3].astype(f32)).astype(bf16)
    from_ahead = lax.ppermute(to_back, "head", cyclic(4, 3))
    from_back = lax.ppermute(to_ahead, "head", cyclic(4, 1))
    mine = parts[0].astype(f32) + from_ahead.astype(f32) + from_back.astype(f32)
    return mine + jnp.where((me == 0) | (me == 3), far_wide, 0.0)


def is_power(count):
    return count & (count - 1) == 0


def gather_small(values):
    held = values[None]
    for axis in ("head", "blk"):
        count = lax.axis_size(axis)
        if not is_power(count):
            held = lax.all_gather(held, axis, axis=0, tiled=False)
        else:
            me = lax.axis_index(axis)
            held = held[None]
            bit = 1
            while bit < count:
                other = lax.ppermute(held, axis, [(i, i ^ bit) for i in range(count)])
                low = jnp.concatenate([held, other])
                high = jnp.concatenate([other, held])
                held = jnp.where((me // bit) % 2 == 0, low, high)
                bit *= 2
        if axis == "head":
            held = held.reshape(count, -1)
    return held


def scatter_small(values):
    for axis in ("blk", "head"):
        count = lax.axis_size(axis)
        if not is_power(count):
            values = lax.psum_scatter(values, axis, scatter_dimension=0, tiled=False)
            continue
        me = lax.axis_index(axis)
        bit = count // 2
        while bit >= 1:
            upper = (me // bit) % 2 == 1
            low, high = values[:bit], values[bit:]
            kept, sent = jnp.where(upper, high, low), jnp.where(upper, low, high)
            values = kept + lax.ppermute(sent, axis, [(i, i ^ bit) for i in range(count)])
            bit //= 2
        values = values[0]
    return values


def lane_low(shape):
    return lax.broadcasted_iota(jnp.int32, shape, 1) < HD


def swap_halves(tile):
    return pltpu.roll(tile, HD, 1)


def pair_up(first, second):
    low = lane_low(first.shape)
    return (
        jnp.where(low, first, swap_halves(second)),
        jnp.where(low, swap_halves(first), second),
    )


def project_kernel(slots, *refs):
    x_refs = refs[:slots]
    gain_ref, wq_ref, wk_ref, wv_ref, normed_ref, packed_ref = refs[slots:]
    rows = slots * SPAN

    @pl.when(pl.program_id(0) == 0)
    def _():
        for s in range(slots):
            wide = x_refs[s][...].astype(f32)
            normed = wide * rms_scale(wide) * gain_ref[...]
            normed_ref[s * SPAN : (s + 1) * SPAN, :] = normed.astype(bf16)

    normed = normed_ref[...]
    query = dot_nn(normed, wq_ref[...])
    key = dot_nn(normed, wk_ref[...])
    value = dot_nn(normed, wv_ref[...])
    half = rows // 2
    for pair in range(query.shape[1] // LANES):
        cols = slice(pair * LANES, (pair + 1) * LANES)
        both = pair_up(value[:, cols], key[:, cols])
        queries = pair_up(query[:half, cols], query[half:, cols])
        for member in range(2):
            packed_ref[2 * pair + member, :rows, :] = both[member].astype(bf16)
            packed_ref[2 * pair + member, rows:, :] = queries[member].astype(bf16)


def project(x_slots, gain, weights):
    slots = len(x_slots)
    rows, depth = slots * SPAN, x_slots[0].shape[1]
    width = weights.shape[1] // 3
    heads = width // HD
    tile = min(width, 256)
    steps = width // tile
    whole = pl.BlockSpec((SPAN, depth), lambda j: (0, 0))

    def columns(part):
        return pl.BlockSpec((depth, tile), lambda j: (0, part * steps + j))

    return pl.pallas_call(
        functools.partial(project_kernel, slots),
        grid=(steps,),
        in_specs=[whole] * slots
        + [pl.BlockSpec((1, depth), lambda j: (0, 0)), columns(0), columns(1), columns(2)],
        out_specs=[
            pl.BlockSpec((rows, depth), lambda j: (0, 0)),
            pl.BlockSpec((tile // HD, rows + rows // 2, LANES), lambda j: (j, 0, 0)),
        ],
        out_shape=[
            jax.ShapeDtypeStruct((rows, depth), bf16),
            jax.ShapeDtypeStruct((heads, rows + rows // 2, LANES), bf16),
        ],
        compiler_params=pltpu.CompilerParams(vmem_limit_bytes=40 * MIB),
        cost_estimate=pl.CostEstimate(
            flops=6 * rows * depth * width, bytes_accessed=6 * depth * width, transcendentals=0
        ),
        name="project",
    )(*x_slots, gain, weights, weights, weights)


def place_of(order_ref, info_ref, source, slot, slots):
    z = info_ref[0]
    return order_ref[source * slots + lax.rem(z - slot + slots, slots)]


def dyn(start, size, multiple):
    return pl.ds(pl.multiple_of(start, multiple), size)


def fill_table(bias_ref, table_ref):
    left = OFF - SPAN
    right = left + MID_BLOCKS * SPAN
    table_ref[:left, :] = jnp.broadcast_to(bias_ref[MID_BLOCKS : MID_BLOCKS + 1, :BQ], (left, BQ))
    table_ref[right:, :] = jnp.broadcast_to(
        bias_ref[MID_BLOCKS + 1 : MID_BLOCKS + 2, :BQ], (TABLE_ROWS - right, BQ)
    )
    for c in range(MID_BLOCKS):
        spread = jnp.broadcast_to(bias_ref[c : c + 1, :], (SPAN, WIDE))
        rolled = pltpu.roll(spread, 0, 1, stride=1, stride_axis=0)
        table_ref[left + c * SPAN : left + (c + 1) * SPAN, :] = rolled[:, :BQ]


def block_range(ends_ref, q0, total):
    count = ends_ref.shape[0]
    start, end, cut = jnp.int32(0), jnp.int32(total), jnp.bool_(False)
    for n in range(count):
        edge = ends_ref[n]
        start = jnp.where(edge <= q0, edge, start)
        cut = cut | ((edge > q0) & (edge < q0 + BQ))
    for n in range(count - 1, -1, -1):
        edge = ends_ref[n]
        end = jnp.where(edge >= q0 + BQ, edge, end)
    first = lax.div(start, BK)
    last = lax.div(end + BK - 1, BK)
    whole = jnp.logical_not(cut) & (lax.rem(start, BK) == 0) & (lax.rem(end, BK) == 0)
    near = jnp.clip(lax.div(jnp.maximum(q0 - SPAN, 0), BK), first, last)
    beyond = jnp.clip(lax.div(q0 + BQ + SPAN + BK - 1, BK), first, last)
    return first, near, beyond, last, whole


def same_sequence(ends_ref, k0, q0):
    key_place = k0 + lax.broadcasted_iota(jnp.int32, (BK, 1), 0)
    query_place = q0 + lax.broadcasted_iota(jnp.int32, (1, BQ), 1)
    key_seg = jnp.zeros((BK, 1), jnp.int32)
    query_seg = jnp.zeros((1, BQ), jnp.int32)
    for n in range(ends_ref.shape[0]):
        key_seg = key_seg + jnp.where(key_place >= ends_ref[n], 1, 0)
        query_seg = query_seg + jnp.where(query_place >= ends_ref[n], 1, 0)
    return key_seg == query_seg


def table_start(k0, q0):
    return pl.multiple_of(jnp.clip(k0 - q0, -(BK + 2 * SPAN), BQ + 2 * SPAN) + OFF, SPAN)


def sort_blocks(order_ref, info_ref, x_ref, slots, keep):
    sources = x_ref.shape[0]
    half = slots // 2
    high = jnp.logical_not(lane_low((SPAN, LANES)))
    for source in range(sources):
        for pair in range(half):
            packed = x_ref[
                source, (slots + pair) * SPAN : (slots + pair + 1) * SPAN, :
            ].astype(f32)
            queries = (swap_halves(packed), packed)
            for member in range(2):
                slot = pair + member * half
                place = place_of(order_ref, info_ref, source, slot, slots) * SPAN
                both = x_ref[source, slot * SPAN : (slot + 1) * SPAN, :]
                keep(place, both, jnp.where(high, queries[member], 0.0).astype(bf16))


def attend_kernel(
    slots, order_ref, ends_ref, info_ref, x_ref, bias_ref, mixed_ref, exact_ref, lse_ref,
    both_ref, query_ref, turned_ref, table_ref, held_ref,
):
    total = both_ref.shape[0]
    parted = info_ref.shape[0] > 3

    def keep(place, both, query):
        both_ref[dyn(place, SPAN, SPAN), :] = both
        query_ref[dyn(place, SPAN, SPAN), :] = query
        turned = both.astype(f32).T
        turned_ref[:, dyn(place, SPAN, SPAN)] = turned[:HD, :].astype(bf16)

    sort_blocks(order_ref, info_ref, x_ref, slots, keep)
    fill_table(bias_ref, table_ref)
    if parted:
        held_ref[...] = jnp.zeros_like(held_ref)
        exact_ref[...] = jnp.zeros_like(exact_ref)
        lse_ref[...] = jnp.zeros_like(lse_ref)
    left_bias = bias_ref[MID_BLOCKS : MID_BLOCKS + 1, :BQ]
    right_bias = bias_ref[MID_BLOCKS + 1 : MID_BLOCKS + 2, :BQ]
    start_state = (
        jnp.full((1, BQ), masked_score, f32),
        jnp.zeros((1, BQ), f32),
        jnp.zeros((HD, BQ), f32),
    )

    def one_block(block, unused):
        q0 = block * BQ
        first, near, beyond, last, whole = block_range(ends_ref, q0, total)
        query = query_ref[dyn(q0, BQ, BQ), :]

        def step(kind, tile, state):
            peak, mass, mix = state
            k0 = tile * BK
            scores = dot_nt(both_ref[dyn(k0, BK, BK), :], query)
            constant = 0.0
            if kind in ("near", "cut"):
                scores = scores + table_ref[pl.ds(table_start(k0, q0), BK), :]
            elif kind == "left":
                constant = left_bias
            else:
                constant = right_bias
            if kind == "cut":
                same = same_sequence(ends_ref, k0, q0)
                scores = jnp.where(same, scores, masked_score)
            new_peak = jnp.maximum(peak, jnp.max(scores, axis=0, keepdims=True) + constant)
            weights = jnp.exp(scores - (new_peak - constant))
            if kind == "cut":
                weights = jnp.where(same, weights, 0.0)
            rescale = jnp.exp(peak - new_peak)
            mass = mass * rescale + jnp.sum(weights, axis=0, keepdims=True)
            turned = turned_ref[:, dyn(k0, BK, BK)]
            mix = mix * rescale + dot_nn(turned, weights.astype(bf16))
            return (new_peak, mass, mix)

        def finish(state):
            peak, mass, mix = state
            exact = mix / mass
            exact_ref[:, dyn(q0, BQ, BQ)] = exact
            lse_ref[:, dyn(q0, BQ, BQ)] = peak + jnp.log(mass)
            padded = jnp.concatenate([exact, exact], axis=0)
            held_ref[dyn(q0, BQ, BQ), :] = padded.T

        @pl.when(whole)
        def _():
            state = lax.fori_loop(first, near, functools.partial(step, "left"), start_state)
            state = lax.fori_loop(near, beyond, functools.partial(step, "near"), state)
            finish(lax.fori_loop(beyond, last, functools.partial(step, "right"), state))

        @pl.when(jnp.logical_not(whole))
        def _():
            finish(lax.fori_loop(first, last, functools.partial(step, "cut"), start_state))

        return unused

    lax.fori_loop(info_ref[1], info_ref[2], one_block, 0)
    half = slots // 2
    low = lane_low((SPAN, LANES))
    for source in range(x_ref.shape[0]):
        for pair in range(half):
            places = [
                place_of(order_ref, info_ref, source, pair + m * half, slots) * SPAN
                for m in range(2)
            ]
            tiles = [held_ref[dyn(place, SPAN, SPAN), :] for place in places]
            mixed_ref[source, pair * SPAN : (pair + 1) * SPAN, :] = jnp.where(
                low, tiles[0], tiles[1]
            ).astype(bf16)


def vmem(shape, dtype):
    return pltpu.VMEM(shape, dtype)


def smem_spec():
    return pl.BlockSpec(memory_space=pltpu.SMEM)


def vmem_spec():
    return pl.BlockSpec(memory_space=pltpu.VMEM)


def attention_vmem(total):
    return int(min(58, 16 + 44 * (total / 16384)) * MIB)


def attend(order, ends, info, swapped, bias_rows, slots):
    sources = swapped.shape[0]
    total = sources * slots * SPAN
    return pl.pallas_call(
        functools.partial(attend_kernel, slots),
        in_specs=[smem_spec()] * 3 + [vmem_spec()] * 2,
        out_specs=[vmem_spec()] * 3,
        out_shape=[
            jax.ShapeDtypeStruct((sources, slots * SPAN // 2, LANES), bf16),
            jax.ShapeDtypeStruct((HD, total), f32),
            jax.ShapeDtypeStruct((1, total), f32),
        ],
        scratch_shapes=[
            vmem((total, LANES), bf16),
            vmem((total, LANES), bf16),
            vmem((HD, total), bf16),
            vmem((TABLE_ROWS, BQ), f32),
            vmem((total, LANES), f32),
        ],
        compiler_params=pltpu.CompilerParams(vmem_limit_bytes=attention_vmem(total)),
        cost_estimate=pl.CostEstimate(
            flops=total * total * 128, bytes_accessed=total * 2048, transcendentals=total * total // 2
        ),
        name="attend",
    )(order, ends, info, swapped, bias_rows)


def unroll_rows(tile):
    row = lax.broadcasted_iota(jnp.int32, tile.shape, 0)
    bit = 1
    while bit < tile.shape[0]:
        moved = pltpu.roll(tile, tile.shape[1] - bit, 1)
        tile = jnp.where((row // bit) % 2 == 1, moved, tile)
        bit *= 2
    return tile


def attend_back_kernel(
    slots, bucket_count, order_ref, ends_ref, info_ref, x_ref, mixed_ref, exact_ref, lse_ref,
    bias_ref, bucket_ref, grad_ref,
    both_ref, query_ref, back_ref, turned_ref, table_ref, d_table_ref, d_both_ref, d_query_ref,
    far_ref,
):
    total = both_ref.shape[0]
    sources = x_ref.shape[0]
    half = slots // 2
    low = lane_low((SPAN, LANES))

    def keep(place, both, query):
        both_ref[dyn(place, SPAN, SPAN), :] = both
        query_ref[dyn(place, SPAN, SPAN), :] = query
        turned = both.astype(f32).T
        turned_ref[:HD, dyn(place, SPAN, SPAN)] = turned[HD:, :].astype(bf16)

    sort_blocks(order_ref, info_ref, x_ref, slots, keep)
    for source in range(sources):
        for pair in range(half):
            packed = mixed_ref[source, pair * SPAN : (pair + 1) * SPAN, :].astype(f32)
            for member, tile in enumerate((packed, swap_halves(packed))):
                place = place_of(order_ref, info_ref, source, pair + member * half, slots) * SPAN
                back_ref[dyn(place, SPAN, SPAN), :] = jnp.where(low, tile, 0.0).astype(bf16)
    fill_table(bias_ref, table_ref)
    tail = lax.broadcasted_iota(jnp.int32, (KT_ROWS - HD, total), 0)
    turned_ref[HD:, :] = jnp.where(tail == 0, 1.0, 0.0).astype(bf16)
    d_table_ref[...] = jnp.zeros_like(d_table_ref)
    d_both_ref[...] = jnp.zeros_like(d_both_ref)
    far_ref[...] = jnp.zeros_like(far_ref)
    if info_ref.shape[0] > 3:
        d_query_ref[...] = jnp.zeros_like(d_query_ref)
    left_bias = bias_ref[MID_BLOCKS : MID_BLOCKS + 1, :BQ]
    right_bias = bias_ref[MID_BLOCKS + 1 : MID_BLOCKS + 2, :BQ]

    def one_block(block, unused):
        q0 = block * BQ
        first, near, beyond, last, whole = block_range(ends_ref, q0, total)
        query = query_ref[dyn(q0, BQ, BQ), :]
        back = back_ref[dyn(q0, BQ, BQ), :]
        lse = lse_ref[:, dyn(q0, BQ, BQ)]
        turned_back = back.astype(f32).T[:HD, :]
        delta = jnp.sum(turned_back * exact_ref[:, dyn(q0, BQ, BQ)], axis=0, keepdims=True)

        def step(kind, tile, d_turned):
            k0 = tile * BK
            keys = dyn(k0, BK, BK)
            both = both_ref[keys, :]
            scores = dot_nt(both, query)
            if kind in ("near", "cut"):
                rows = pl.ds(table_start(k0, q0), BK)
                weights = jnp.exp(scores + table_ref[rows, :] - lse)
            elif kind == "left":
                weights = jnp.exp(scores - (lse - left_bias))
            else:
                weights = jnp.exp(scores - (lse - right_bias))
            if kind == "cut":
                weights = jnp.where(same_sequence(ends_ref, k0, q0), weights, 0.0)
            d_probs = dot_nt(both, back)
            d_scores = (weights * (d_probs - delta)).astype(bf16)
            if kind in ("near", "cut"):
                d_table_ref[rows, :] = d_table_ref[rows, :] + d_scores.astype(f32)
            d_both_ref[keys, :] = (
                d_both_ref[keys, :] + dot_nn(weights.astype(bf16), back) + dot_nn(d_scores, query)
            )
            return d_turned + dot_nn(turned_ref[:, keys], d_scores)

        def finish(d_turned):
            top = d_turned[:HD, :]
            d_query_ref[dyn(q0, BQ, BQ), :] = jnp.concatenate([top, top], axis=0).T

        zero = jnp.zeros((KT_ROWS, BQ), f32)

        @pl.when(whole)
        def _():
            at_left = lax.fori_loop(first, near, functools.partial(step, "left"), zero)
            far_ref[0:1, :] = far_ref[0:1, :] + at_left[HD : HD + 1, :]
            at_near = lax.fori_loop(near, beyond, functools.partial(step, "near"), at_left)
            at_right = lax.fori_loop(beyond, last, functools.partial(step, "right"), zero)
            far_ref[1:2, :] = far_ref[1:2, :] + at_right[HD : HD + 1, :]
            finish(at_near + at_right)

        @pl.when(jnp.logical_not(whole))
        def _():
            finish(lax.fori_loop(first, last, functools.partial(step, "cut"), zero))

        return unused

    lax.fori_loop(info_ref[1], info_ref[2], one_block, 0)

    left = OFF - SPAN
    right = left + MID_BLOCKS * SPAN
    sums = []
    for c in range(MID_BLOCKS):
        tile = d_table_ref[left + c * SPAN : left + (c + 1) * SPAN, :]
        wide = jnp.concatenate([tile, jnp.zeros((SPAN, WIDE - BQ), f32)], axis=1)
        sums.append(jnp.sum(unroll_rows(wide), axis=0, keepdims=True))
    lefts = far_ref[0:1, :] + jnp.sum(d_table_ref[:left, :], axis=0, keepdims=True)
    rights = far_ref[1:2, :] + jnp.sum(d_table_ref[right:, :], axis=0, keepdims=True)
    blank = jnp.zeros((1, WIDE - BQ), f32)
    sums.append(jnp.concatenate([lefts, blank], axis=1))
    sums.append(jnp.concatenate([rights, blank], axis=1))
    sums = jnp.concatenate(sums, axis=0)
    buckets = bucket_ref[: MID_BLOCKS + 2, :]
    per_source = bucket_count // sources
    lane = lax.broadcasted_iota(jnp.int32, (1, LANES), 1)
    row = lax.broadcasted_iota(jnp.int32, (EXTRA, LANES), 0)
    for source in range(sources):
        line = jnp.zeros((1, LANES), f32)
        for j in range(per_source):
            picked = jnp.where(buckets == source * per_source + j, sums, 0.0)
            one = jnp.sum(jnp.sum(picked, axis=0, keepdims=True), axis=1, keepdims=True)
            line = jnp.where(lane == j, one, line)
        upper = line.astype(bf16).astype(f32)
        rest = line - upper
        grad_ref[source, 3 * half * SPAN :, :] = jnp.where(
            row == 0, upper, jnp.where(row == 1, rest, 0.0)
        ).astype(bf16)

    for source in range(sources):
        for pair in range(half):
            tiles = []
            for member in range(2):
                slot = pair + member * half
                place = place_of(order_ref, info_ref, source, slot, slots) * SPAN
                grad_ref[source, slot * SPAN : (slot + 1) * SPAN, :] = d_both_ref[
                    dyn(place, SPAN, SPAN), :
                ].astype(bf16)
                tiles.append(d_query_ref[dyn(place, SPAN, SPAN), :])
            grad_ref[source, (slots + pair) * SPAN : (slots + pair + 1) * SPAN, :] = jnp.where(
                low, tiles[0], tiles[1]
            ).astype(bf16)


def attend_back(
    order, ends, info, swapped, mixed_grad, exact, lse, bias_rows, bucket_rows, slots, bucket_count
):
    sources = swapped.shape[0]
    total = sources * slots * SPAN
    return pl.pallas_call(
        functools.partial(attend_back_kernel, slots, bucket_count),
        in_specs=[smem_spec()] * 3 + [vmem_spec()] * 6,
        out_specs=vmem_spec(),
        out_shape=jax.ShapeDtypeStruct((sources, slots * SPAN * 3 // 2 + EXTRA, LANES), bf16),
        scratch_shapes=[
            vmem((total, LANES), bf16),
            vmem((total, LANES), bf16),
            vmem((total, LANES), bf16),
            vmem((KT_ROWS, total), bf16),
            vmem((TABLE_ROWS, BQ), f32),
            vmem((TABLE_ROWS, BQ), f32),
            vmem((total, LANES), f32),
            vmem((total, LANES), f32),
            vmem((8, BQ), f32),
        ],
        compiler_params=pltpu.CompilerParams(vmem_limit_bytes=attention_vmem(total)),
        cost_estimate=pl.CostEstimate(
            flops=total * total * 320, bytes_accessed=total * 3072, transcendentals=total * total // 2
        ),
        name="attend_back",
    )(order, ends, info, swapped, mixed_grad, exact, lse, bias_rows, bucket_rows)


def out_kernel(slots, packed_ref, weight_ref, mix_ref, part_ref):
    heads = packed_ref.shape[0]
    half = slots * SPAN // 2

    @pl.when(pl.program_id(0) == 0)
    def _():
        for pair in range(heads // 2):
            first = packed_ref[2 * pair].astype(f32)
            second = packed_ref[2 * pair + 1].astype(f32)
            top, bottom = pair_up(first, second)
            cols = slice(pair * LANES, (pair + 1) * LANES)
            mix_ref[:half, cols] = top.astype(bf16)
            mix_ref[half:, cols] = bottom.astype(bf16)

    part = dot_nn(mix_ref[...], weight_ref[...]).astype(bf16)
    for s in range(slots):
        part_ref[s] = part[s * SPAN : (s + 1) * SPAN]


def out_project(packed, weight, slots):
    heads = packed.shape[0]
    rows, width, depth = slots * SPAN, heads * HD, weight.shape[1]
    tile = 512
    return pl.pallas_call(
        functools.partial(out_kernel, slots),
        grid=(depth // tile,),
        in_specs=[
            pl.BlockSpec(packed.shape, lambda j: (0, 0, 0)),
            pl.BlockSpec((width, tile), lambda j: (0, j)),
        ],
        out_specs=[
            pl.BlockSpec((rows, width), lambda j: (0, 0)),
            pl.BlockSpec((slots, SPAN, tile), lambda j: (0, 0, j)),
        ],
        out_shape=[
            jax.ShapeDtypeStruct((rows, width), bf16),
            jax.ShapeDtypeStruct((slots, SPAN, depth), bf16),
        ],
        compiler_params=pltpu.CompilerParams(vmem_limit_bytes=32 * MIB),
        cost_estimate=pl.CostEstimate(
            flops=2 * rows * depth * width, bytes_accessed=4 * depth * width, transcendentals=0
        ),
        name="out_project",
    )(packed, weight)


def feed_kernel(slots, *refs):
    normed_refs, grad_refs = refs[:slots], refs[slots : 2 * slots]
    both_ref, down_ref, rows_ref, rows_grad_ref, active_ref, d_both_ref = refs[2 * slots :]

    @pl.when(pl.program_id(0) == 0)
    def _():
        for s in range(slots):
            rows_ref[s * SPAN : (s + 1) * SPAN, :] = normed_refs[s][...]
            rows_grad_ref[s * SPAN : (s + 1) * SPAN, :] = grad_refs[s][...]

    tile = down_ref.shape[0]
    pre = dot_nn(rows_ref[...], both_ref[...])
    d_hidden = dot_nt(rows_grad_ref[...], down_ref[...])
    gate, up = pre[:, :tile], pre[:, tile:]
    scale, cubic = 0.7978845608028654, 0.044715
    square = gate * gate
    bent = jnp.tanh(scale * (gate + cubic * square * gate))
    half = 0.5 * (1.0 + bent)
    gelu = gate * half
    slope = half + 0.5 * gate * (1.0 - bent * bent) * (scale * (1.0 + 3.0 * cubic * square))
    active_ref[...] = (gelu * up).astype(bf16)
    d_both_ref[:, :tile] = (d_hidden * up * slope).astype(bf16)
    d_both_ref[:, tile:] = (d_hidden * gelu).astype(bf16)


def feed_tile(width):
    return 256 if width % 256 == 0 else 128


def feed(normed_slots, grad_slots, both, down):
    slots = len(normed_slots)
    rows, depth, width = slots * SPAN, both.shape[0], down.shape[0]
    tile = feed_tile(width)
    whole = pl.BlockSpec((SPAN, depth), lambda j: (0, 0))
    rows_spec = pl.BlockSpec((rows, depth), lambda j: (0, 0))
    return pl.pallas_call(
        functools.partial(feed_kernel, slots),
        grid=(width // tile,),
        in_specs=[whole] * (2 * slots)
        + [
            pl.BlockSpec((depth, 2 * tile), lambda j: (0, j)),
            pl.BlockSpec((tile, depth), lambda j: (j, 0)),
        ],
        out_specs=[
            rows_spec,
            rows_spec,
            pl.BlockSpec((rows, tile), lambda j: (0, j)),
            pl.BlockSpec((rows, 2 * tile), lambda j: (0, j)),
        ],
        out_shape=[
            jax.ShapeDtypeStruct((rows, depth), bf16),
            jax.ShapeDtypeStruct((rows, depth), bf16),
            jax.ShapeDtypeStruct((rows, width), bf16),
            jax.ShapeDtypeStruct((rows, 2 * width), bf16),
        ],
        compiler_params=pltpu.CompilerParams(vmem_limit_bytes=56 * MIB),
        cost_estimate=pl.CostEstimate(
            flops=6 * rows * depth * width,
            bytes_accessed=6 * depth * width,
            transcendentals=rows * width,
        ),
        name="feed",
    )(*normed_slots, *grad_slots, both, down)


def mix_back_kernel(slots, *refs):
    grad_refs = refs[:slots]
    weight_ref, rows_ref, packed_ref = refs[slots:]
    half = slots * SPAN // 2

    @pl.when(pl.program_id(0) == 0)
    def _():
        for s in range(slots):
            rows_ref[s * SPAN : (s + 1) * SPAN, :] = grad_refs[s][...]

    mixed = dot_nt(rows_ref[...], weight_ref[...])
    for pair in range(mixed.shape[1] // LANES):
        cols = slice(pair * LANES, (pair + 1) * LANES)
        both = pair_up(mixed[:half, cols], mixed[half:, cols])
        for member in range(2):
            packed_ref[2 * pair + member] = both[member].astype(bf16)


def mix_back(grad_slots, weight):
    slots = len(grad_slots)
    width, depth = weight.shape
    rows = slots * SPAN
    tile = min(width, 256)
    whole = pl.BlockSpec((SPAN, depth), lambda j: (0, 0))
    return pl.pallas_call(
        functools.partial(mix_back_kernel, slots),
        grid=(width // tile,),
        in_specs=[whole] * slots + [pl.BlockSpec((tile, depth), lambda j: (j, 0))],
        out_specs=[
            pl.BlockSpec((rows, depth), lambda j: (0, 0)),
            pl.BlockSpec((tile // HD, rows // 2, LANES), lambda j: (j, 0, 0)),
        ],
        out_shape=[
            jax.ShapeDtypeStruct((rows, depth), bf16),
            jax.ShapeDtypeStruct((width // HD, rows // 2, LANES), bf16),
        ],
        compiler_params=pltpu.CompilerParams(vmem_limit_bytes=32 * MIB),
        cost_estimate=pl.CostEstimate(
            flops=2 * rows * depth * width, bytes_accessed=4 * depth * width, transcendentals=0
        ),
        name="mix_back",
    )(*grad_slots, weight)


def project_back_kernel(slots, packed_ref, weight_ref, grads_ref, part_ref):
    heads = packed_ref.shape[0]
    rows = slots * SPAN
    half = rows // 2
    width = heads * HD

    @pl.when(pl.program_id(0) == 0)
    def _():
        for pair in range(heads // 2):
            start = pair * LANES
            tiles = [packed_ref[2 * pair + m].astype(f32) for m in range(2)]
            value, key = pair_up(tiles[0][:rows], tiles[1][:rows])
            top, bottom = pair_up(tiles[0][rows : rows + half], tiles[1][rows : rows + half])
            grads_ref[:half, start : start + LANES] = top.astype(bf16)
            grads_ref[half:, start : start + LANES] = bottom.astype(bf16)
            grads_ref[:, width + start : width + start + LANES] = key.astype(bf16)
            grads_ref[:, 2 * width + start : 2 * width + start + LANES] = value.astype(bf16)

    part = dot_nt(grads_ref[...], weight_ref[...]).astype(bf16)
    for s in range(slots):
        part_ref[s] = part[s * SPAN : (s + 1) * SPAN]


def project_back(packed, weights, slots):
    heads = packed.shape[0]
    depth, width = weights.shape
    rows = slots * SPAN
    tile = 512
    return pl.pallas_call(
        functools.partial(project_back_kernel, slots),
        grid=(depth // tile,),
        in_specs=[
            pl.BlockSpec(packed.shape, lambda j: (0, 0, 0)),
            pl.BlockSpec((tile, width), lambda j: (j, 0)),
        ],
        out_specs=[
            pl.BlockSpec((rows, width), lambda j: (0, 0)),
            pl.BlockSpec((slots, SPAN, tile), lambda j: (0, 0, j)),
        ],
        out_shape=[
            jax.ShapeDtypeStruct((rows, width), bf16),
            jax.ShapeDtypeStruct((slots, SPAN, depth), bf16),
        ],
        compiler_params=pltpu.CompilerParams(vmem_limit_bytes=40 * MIB),
        cost_estimate=pl.CostEstimate(
            flops=2 * rows * depth * width, bytes_accessed=2 * depth * width, transcendentals=0
        ),
        name="project_back",
    )(packed, weights)


def bucket_lines(bucket_of):
    count = bucket_of.shape[0]
    turned = bucket_of[::-1]
    pad = 5 * WIDE // 4
    padded = jnp.concatenate(
        [
            jnp.broadcast_to(turned[:1], (pad,)),
            turned,
            jnp.broadcast_to(turned[-1:], (pad,)),
        ]
    )
    zero_at = pad + count // 2
    keep = BQ + HD
    rows = []
    for c in range(MID_BLOCKS):
        base = zero_at - (c - 1) * SPAN
        rows.append(
            jnp.concatenate([padded[base : base + keep], padded[base - (WIDE - keep) : base]])
        )
    rows.append(jnp.broadcast_to(bucket_of[:1], (WIDE,)))
    rows.append(jnp.broadcast_to(bucket_of[-1:], (WIDE,)))
    spare = 8 * ((MID_BLOCKS + 2 + 7) // 8) - (MID_BLOCKS + 2)
    return jnp.concatenate([jnp.stack(rows), jnp.full((spare, WIDE), -1, bucket_of.dtype)])


def interleave(first, second, tile):
    rows = first.shape[0]
    return jnp.concatenate(
        [first.reshape(rows, -1, 1, tile), second.reshape(rows, -1, 1, tile)], axis=2
    ).reshape(rows, -1)


def on_device(
    tokens,
    lengths,
    block_order,
    bucket_of,
    gain_attn,
    w_query,
    w_key,
    w_value,
    w_out,
    bias_table,
    gain_ffn,
    w_gate,
    w_up,
    w_down,
    cotangent,
):
    blk_count, slots = lax.axis_size("blk"), lax.axis_size("head")
    blk_spot, head_spot = lax.axis_index("blk"), lax.axis_index("head")
    depth = tokens.shape[1]
    width = w_query.shape[1]
    heads = width // HD
    shares = blk_count // heads
    table_rows, table_heads = bias_table.shape
    bucket_count = table_rows * blk_count
    total = blk_count * slots * SPAN
    gain_size = gain_attn.shape[0]
    tile = feed_tile(w_gate.shape[1])

    token_slots = gather_slots(tokens)
    small = gather_small(
        jnp.concatenate([gain_attn, gain_ffn, bias_table.astype(f32).reshape(-1)])
    )
    full_qkv = lax.all_gather(
        jnp.concatenate([w_query, w_key, w_value], axis=1), "blk", axis=0, tiled=True
    )
    full_out = lax.all_gather(w_out, "blk", axis=1, tiled=True)
    full_both = lax.all_gather(interleave(w_gate, w_up, tile), "blk", axis=0, tiled=True)
    full_down = lax.all_gather(w_down, "blk", axis=1, tiled=True)
    gain_one = small[:, :, :gain_size].reshape(1, depth)
    gain_two = small[:, :, gain_size : 2 * gain_size].reshape(1, depth)

    tables = lax.dynamic_index_in_dim(small, head_spot, 1, False)[:, 2 * gain_size :]
    tables = tables.reshape(bucket_count, table_heads)
    my_head = blk_spot // shares
    my_bias = lax.dynamic_index_in_dim(tables, my_head, 1, False)
    bucket_rows = bucket_lines(bucket_of)
    bias_rows = jnp.sum(
        jnp.where(
            bucket_rows[None] == jnp.arange(bucket_count, dtype=jnp.int32)[:, None, None],
            my_bias[:, None, None],
            0.0,
        ),
        axis=0,
    )
    ends = jnp.cumsum(lengths).astype(jnp.int32)
    per_share = total // BQ // shares
    start = (blk_spot % shares) * per_share
    info = [head_spot, start, start + per_share] + ([start] if shares > 1 else [])
    info = jnp.stack([jnp.asarray(item, jnp.int32) for item in info])

    def swap(values):
        return lax.all_to_all(values, "blk", 0, 0, tiled=True)

    def to_heads(values):
        return swap(values if shares == 1 else jnp.repeat(values, shares, axis=0))

    def to_rows(values):
        values = swap(values)
        if shares == 1:
            return values
        values = values.reshape((heads, shares) + values.shape[1:])
        return jnp.sum(values.astype(f32), axis=1).astype(bf16)

    normed_one, packed = project(token_slots, gain_one, full_qkv)
    swapped = to_heads(packed)
    mixed, exact, lse = attend(block_order, ends, info, swapped, bias_rows, slots)
    attn_mix, out_parts = out_project(to_rows(mixed), full_out, slots)
    tokens_wide = tokens.astype(f32)
    hidden_one = tokens_wide + sum_slots([out_parts[s] for s in range(slots)])
    rstd_two = rms_scale(hidden_one)
    normed_two = (hidden_one * rstd_two * gain_two).astype(bf16)

    grad_slots = gather_slots(cotangent)
    normed_slots = gather_slots(normed_two)
    rows_two, rows_grad, active, d_both = feed(normed_slots, grad_slots, full_both, full_down)
    d_parts = dot_nt(d_both, full_both).astype(bf16)
    d_normed_two = sum_slots([d_parts[s * SPAN : (s + 1) * SPAN] for s in range(slots)])
    down_parts = dot_nn(active, full_down).astype(bf16)
    output = hidden_one + sum_slots([down_parts[s * SPAN : (s + 1) * SPAN] for s in range(slots)])
    grad_both = lax.psum_scatter(
        dot_tn(rows_two, d_both).astype(bf16), "blk", scatter_dimension=0, tiled=True
    )
    grad_down = lax.psum_scatter(
        dot_tn(active, rows_grad).astype(bf16), "blk", scatter_dimension=1, tiled=True
    )
    d_source_two, gain_part_two = norm_back(d_normed_two, hidden_one, rstd_two, gain_two)
    d_hidden_one = cotangent.astype(f32) + d_source_two

    attn_slots = gather_slots(d_hidden_one.astype(bf16))
    rows_attn, mix_grads = mix_back(attn_slots, full_out)
    grad_out = lax.psum_scatter(
        dot_tn(attn_mix, rows_attn).astype(bf16), "blk", scatter_dimension=1, tiled=True
    )
    grads = attend_back(
        block_order, ends, info, swapped, to_heads(mix_grads), exact, lse, bias_rows, bucket_rows,
        slots, bucket_count,
    )
    grads = swap(grads)
    extra = grads[:, -EXTRA : -EXTRA + 2, :table_rows].astype(f32).sum(axis=1)
    grad_table = extra.reshape(heads, shares, table_rows).sum(axis=1).T
    if shares > 1:
        grads = grads.reshape((heads, shares) + grads.shape[1:])
        grads = jnp.sum(grads.astype(f32), axis=1).astype(bf16)
    d_qkv, d_parts_one = project_back(grads, full_qkv, slots)
    grad_qkv = lax.psum_scatter(
        dot_tn(normed_one, d_qkv).astype(bf16), "blk", scatter_dimension=0, tiled=True
    )
    d_normed_one = sum_slots([d_parts_one[s] for s in range(slots)])
    d_source_one, gain_part_one = norm_back(
        d_normed_one, tokens_wide, rms_scale(tokens_wide), gain_one
    )
    input_grad = d_hidden_one + d_source_one
    gain_parts = jnp.stack(
        [part.reshape(blk_count, slots, gain_size) for part in (gain_part_one, gain_part_two)],
        axis=2,
    )
    gain_sums = scatter_small(gain_parts)
    grad_qkv = grad_qkv.astype(f32)
    grad_both = grad_both.astype(f32).reshape(grad_both.shape[0], -1, 2, tile)
    return (
        output,
        input_grad,
        gain_sums[0],
        grad_qkv[:, :width],
        grad_qkv[:, width : 2 * width],
        grad_qkv[:, 2 * width :],
        grad_out.astype(f32),
        grad_table,
        gain_sums[1],
        grad_both[:, :, 0].reshape(w_gate.shape),
        grad_both[:, :, 1].reshape(w_up.shape),
        grad_down.astype(f32),
    )


def solution(mesh):
    rows, spread = P(("blk", "head"), None), P(("blk", "head"))
    inward, outward = P("blk", "head"), P("head", "blk")
    in_specs = (
        rows, P(), P(), P(), spread, inward, inward, inward, outward, inward, spread,
        inward, inward, outward, rows,
    )
    out_specs = (
        rows, rows, spread, inward, inward, inward, outward, inward, spread,
        inward, inward, outward,
    )
    return jax.shard_map(
        on_device, mesh=mesh, in_specs=in_specs, out_specs=out_specs, check_vma=False
    )
```

time: 3810 us -> 672 us (0.18)
  local copies, waits for them, and re-layouts: 1460 us -> 46.9 us
  matrix products: 977 us -> 39.6 us
  other arithmetic: 648 us -> 24.9 us
  waiting for transfers between devices: 499 us -> 296 us
  Pallas kernels: 0 us -> 110 us
  blocking collectives: 103 us -> 48.7 us
  starting transfers between devices: 28.4 us -> 81.2 us
  loops' own time: 49.3 us -> 0 us
    dot_general x343 -> x6, matrix products: 977 us -> 39.6 us  [the longest x4 23.8 us: dot_tn(): lax.dot_general(left, right, (((0,), (0,)), ((), ())), preferred_element_...]
    scatter-add x1 -> x0, other arithmetic: 507 us -> none  [on_device(): jax.ops.segment_sum(row_vals, flat_near, num_segments=rel_count)]
    dynamic_update_slice x64 -> x0, local copies, waits for them, and re-layouts: 480 us -> none  [backward_block(): lax.scan(backward_part, carried, split_block(key_blk, value_blk, anchor))]
    reshape x160 -> x5, local copies, waits for them, and re-layouts: 325 us -> 5.08 us  [the longest x1 3.14 us: on_device(): grad_both = grad_both.astype(f32).reshape(grad_both.shape[0], -1, 2, tile)]
    gather x2 -> x0, local copies, waits for them, and re-layouts: 297 us -> none  [on_device(): near_tiles = jnp.take(rel_bias, rel_near, axis=1)]
    all_gather x11 -> x4, waiting for transfers between devices: 224 us -> 0.02 us  [the longest x1 0.02 us: on_device(): full_out = lax.all_gather(w_out, 'blk', axis=1, tiled=True)]
    transpose x65 -> x0, local copies, waits for them, and re-layouts: 185 us -> none  [the longest x64 185 us: scores_of(): jnp.einsum('at,htqk->haqk', picker, near_tiles, precision=lax.Precision.H...]
    while x553 -> x0, local copies, waits for them, and re-layouts: 112 us -> none
  transfers between devices with their start and end apart: 66 -> 44, of which waited for: 38 -> 28; matrix products, arithmetic and copies ran while one was open for 80% -> 10% of each run, Pallas kernels for 0% -> 14%
where the time goes in v1:
time: 672 us; the launch traced here: 663 us
  waiting for transfers between devices  296 us (44%)
  Pallas kernels  110 us (16%)
  starting transfers between devices  81.2 us (12%)
  blocking collectives  48.7 us (7%)
  local copies, waits for them, and re-layouts  46.9 us (7%)
  matrix products  39.6 us (6%)
  other arithmetic  24.9 us (4%)
  between operations  15.1 us (2%)
    reduce_scatter x1, waiting for transfers between devices, on_device(): lax.psum_scatter(dot_tn(rows_two, d_both).astype(bf16), 'blk', scatter_di...  49.3 us
    all_to_all x2, blocking collectives, swap(): return lax.all_to_all(values, 'blk', 0, 0, tiled=True)  48.7 us
    pallas_call x1, Pallas kernels, attend_back(): pl.pallas_call(functools.partial(attend_back_kernel, slots, bucket_count)...  42.2 us
    ppermute x4, waiting for transfers between devices, gather_slots(): ahead_one = lax.ppermute(rows, 'head', cyclic(4, 3))  41.1 us
    pallas_call x1, Pallas kernels, attend(): pl.pallas_call(functools.partial(attend_kernel, slots), in_specs=[smem_sp...  40.1 us
    ppermute x4, waiting for transfers between devices, sum_slots(): far = lax.ppermute(parts[2], 'head', [(0, 1), (1, 3), (2, 0), (3, 2)])  36.5 us
    ppermute x4, waiting for transfers between devices, sum_slots(): from_ahead = lax.ppermute(to_back, 'head', cyclic(4, 3))  35.7 us
    ppermute x5, waiting for transfers between devices, gather_small(): other = lax.ppermute(held, axis, [(i, i ^ bit) for i in range(count)])  30.2 us
  transfers between devices with their start and end apart: 44, of which 28 were waited for; matrix products, arithmetic and copies ran while one was open for 10% of the time, Pallas kernels for 14%

profile of v1, /device:TPU:0, one launch (start us, length us, event | category | flops | bytes accessed | tf_op | source)
XLA Modules:
  0.0 662.9 jit_solution(2313557207717466194)
XLA Ops:
  20.1 22.3 %collective-permute-done.3 = f32[1,1,160]{2,0,1:T(1,128)S(1)} collective-permute-done((f32[1,1,160]{2,0,1:T(1,128)S(1)}, f32[1,1,160]{2,0,1:T(1,128)S(1)}, u32[]{:S(2)}, u32[]{:S(2)}) %collective-permute-start.3) | collective-permute-done | bytes 672 | tf_op jit(solution)/shard_map/ppermute | solution.py:104
  83.4 19.5 %all-to-all-done.x_ref = bf16[8,768,128]{2,1,0:T(8,128)(2,1)S(1)} async-done(((bf16[8,768,128]{2,1,0:T(8,128)(2,1)}), bf16[8,768,128]{2,1,0:T(8,128)(2,1)S(1)}, u32[]{:S(2)}, u32[]{:S(2)}) %all-to-all-start) | async-done | bytes 1572896 | tf_op jit(solution)/shard_map/all_to_all | solution.py:886
  103.0 40.1 %attend.1 = (bf16[8,256,128]{2,1,0:T(8,128)(2,1)}, f32[64,4096]{1,0:T(8,128)S(1)}, f32[1,4096]{1,0:T(1,128)S(1)}) custom-call(s32[32]{0:T(128)S(1)} %copy-done.12, s32[2]{0:T(128)S(1)} %bitcast.73, s32[3]{0:T(128)S(1)} %pad_add_fusion.2.info_ref, bf16[8,768,128]{2,1,0:T(8,128)(2,1)S(1)} %all-to-all-done.x_ref, f32[8,512]{1,0:T(8,128)S(1)} %select_reduce_fusion.bias_ref), custom_call_target="tpu_custom_call" | custom-call | flops 2147483648 | bytes 8388608 | tf_op jit(solution)/shard_map/attend/pallas_call | solution.py:389
  147.6 9.6 %all-to-all-done.1.packed_ref = bf16[8,256,128]{2,1,0:T(8,128)(2,1)S(1)} async-done(((bf16[8,256,128]{2,1,0:T(8,128)(2,1)}), bf16[8,256,128]{2,1,0:T(8,128)(2,1)S(1)}, u32[]{:S(2)}, u32[]{:S(2)}) %all-to-all-start.1) | async-done | bytes 524320 | tf_op jit(solution)/shard_map/all_to_all | solution.py:886
  164.6 9.8 %collective-permute-done.8 = bf16[128,2048]{1,0:T(8,128)(2,1)S(1)} collective-permute-done((bf16[128,2048]{1,0:T(8,128)(2,1)S(1)}, bf16[128,2048]{1,0:T(8,128)(2,1)S(1)}, u32[]{:S(2)}, u32[]{:S(2)}) %collective-permute-start.8) | collective-permute-done | bytes 524320 | tf_op jit(solution)/shard_map/ppermute | solution.py:79
  181.9 20.0 %collective-permute-done.9 = bf16[128,2048]{1,0:T(8,128)(2,1)} collective-permute-done((bf16[128,2048]{1,0:T(8,128)(2,1)}, bf16[128,2048]{1,0:T(8,128)(2,1)}, u32[]{:S(2)}, u32[]{:S(2)}) %collective-permute-start.9) | collective-permute-done | bytes 524320 | tf_op jit(solution)/shard_map/ppermute | solution.py:83
  211.8 12.5 %collective-permute-done.15.refs_7_ = bf16[128,2048]{1,0:T(8,128)(2,1)} collective-permute-done((bf16[128,2048]{1,0:T(8,128)(2,1)S(1)}, bf16[128,2048]{1,0:T(8,128)(2,1)}, u32[]{:S(2)}, u32[]{:S(2)}) %collective-permute-start.15) | collective-permute-done | bytes 524320 | tf_op jit(solution)/shard_map/ppermute | solution.py:65
  229.1 17.6 %collective-permute-done.12.refs_3_ = bf16[128,2048]{1,0:T(8,128)(2,1)S(1)} collective-permute-done((bf16[128,2048]{1,0:T(8,128)(2,1)S(1)}, bf16[128,2048]{1,0:T(8,128)(2,1)S(1)}, u32[]{:S(2)}, u32[]{:S(2)}) %collective-permute-start.12) | collective-permute-done | bytes 524320 | tf_op jit(solution)/shard_map/ppermute | solution.py:65
  247.8 13.1 %collective-permute-start.13 = (bf16[128,2048]{1,0:T(8,128)(2,1)S(1)}, bf16[128,2048]{1,0:T(8,128)(2,1)}, u32[]{:S(2)}, u32[]{:S(2)}) collective-permute-start(bf16[128,2048]{1,0:T(8,128)(2,1)S(1)} %select_select_fusion.2), channel_id=1, source_target_pairs={{1,0},{3,1},{0,2},{2,3},{5,4},{7,5},{4,6},{6,7},{9,8},{11,9},{8,10... | collective-permute-start | bytes 1572872 | tf_op jit(solution)/shard_map/ppermute | solution.py:67
  269.1 14.1 %feed.1 = (bf16[512,2048]{1,0:T(8,128)(2,1)}, bf16[512,2048]{1,0:T(8,128)(2,1)}, bf16[512,1280]{1,0:T(8,128)(2,1)}, bf16[512,2560]{1,0:T(8,128)(2,1)}) custom-call(bf16[128,2048]{1,0:T(8,128)(2,1)} %copy-done.28, bf16[128,2048]{1,0:T(8,128)(2,1)} %copy-done.30, bf16[128,2048]{1,0:T(8,128)(2,1)} %collective-permute-done.13.refs_2_, ...), custom_call_target="tpu_custom_call" | custom-call | flops 8053063680 | bytes 15728640 | tf_op jit(solution)/shard_map/feed/pallas_call | solution.py:667
  283.2 9.2 %convolution_convert_fusion.5 = bf16[512,2048]{1,0:T(8,128)(2,1)S(1)} fusion(bf16[512,2560]{1,0:T(8,128)(2,1)} %get-tuple-element.31, bf16[2048,2560]{1,0:T(8,128)(2,1)} %all-gather.9.cloned.1.call-done.refs_8_), kind=kOutput, calls=%fused_computation.5 | convolution fusion | flops 5369757696 | bytes 15204352 | tf_op jit(solution)/shard_map/dot_general | solution.py:48
  295.4 12.4 %collective-permute-done.20 = bf16[128,2048]{1,0:T(8,128)(2,1)S(1)} collective-permute-done((bf16[128,2048]{1,0:T(8,128)(2,1)S(1)}, bf16[128,2048]{1,0:T(8,128)(2,1)S(1)}, u32[]{:S(2)}, u32[]{:S(2)}) %collective-permute-start.20) | collective-permute-done | bytes 524320 | tf_op jit(solution)/shard_map/ppermute | solution.py:79
  315.6 12.4 %collective-permute-done.21 = bf16[128,2048]{1,0:T(8,128)(2,1)S(1)} collective-permute-done((bf16[128,2048]{1,0:T(8,128)(2,1)S(1)}, bf16[128,2048]{1,0:T(8,128)(2,1)S(1)}, u32[]{:S(2)}, u32[]{:S(2)}) %collective-permute-start.21) | collective-permute-done | bytes 524320 | tf_op jit(solution)/shard_map/ppermute | solution.py:83
  328.0 11.6 %collective-permute-done.22 = bf16[128,2048]{1,0:T(8,128)(2,1)S(1)} collective-permute-done((bf16[128,2048]{1,0:T(8,128)(2,1)S(1)}, bf16[128,2048]{1,0:T(8,128)(2,1)S(1)}, u32[]{:S(2)}, u32[]{:S(2)}) %collective-permute-start.22) | collective-permute-done | bytes 524320 | tf_op jit(solution)/shard_map/ppermute | solution.py:84
  342.6 11.0 %collective-permute-done.24.refs_3_ = bf16[128,2048]{1,0:T(8,128)(2,1)S(1)} collective-permute-done((bf16[128,2048]{1,0:T(8,128)(2,1)S(1)}, bf16[128,2048]{1,0:T(8,128)(2,1)S(1)}, u32[]{:S(2)}, u32[]{:S(2)}) %collective-permute-start.24) | collective-permute-done | bytes 524320 | tf_op jit(solution)/shard_map/ppermute | solution.py:65
  382.4 12.3 %all_to_all.20.mixed_ref = bf16[8,256,128]{2,1,0:T(8,128)(2,1)S(1)} all-to-all(bf16[8,256,128]{2,1,0:T(8,128)(2,1)S(1)} %get-tuple-element.32), channel_id=1, replica_groups=mesh['blk'=8,'head'=4] {'blk'}, dimensions={0} | all-to-all | bytes 1048576 | tf_op jit(solution)/shard_map/all_to_all | solution.py:886
  397.4 42.2 %attend_back.1 = bf16[8,784,128]{2,1,0:T(8,128)(2,1)S(1)} custom-call(s32[32]{0:T(128)S(1)} %copy-done.12, s32[2]{0:T(128)S(1)} %bitcast.74, s32[3]{0:T(128)S(1)} %pad_add_fusion.2.info_ref, bf16[8,768,128]{2,1,0:T(8,128)(2,1)S(1)} %copy-done.8, bf16[8,256,128]{2,1,0:T(8,128)(2,1)S(1)} %all_to_all.20.mixed_ref, f32[64,4096]{1,0:T(8,128)S(1)} %copy-done.16, ...), custom_call_target="tpu_custom_call" | custom-call | flops 5368709120 | bytes 12582912 | tf_op jit(solution)/shard_map/attend_back/pallas_call | solution.py:562
  439.6 36.3 %all_to_all.21.packed_ref = bf16[8,784,128]{2,1,0:T(8,128)(2,1)S(1)} all-to-all(bf16[8,784,128]{2,1,0:T(8,128)(2,1)S(1)} %attend_back.1), channel_id=1, replica_groups=mesh['blk'=8,'head'=4] {'blk'}, dimensions={0} | all-to-all | bytes 3211264 | tf_op jit(solution)/shard_map/all_to_all | solution.py:886
  489.2 9.9 %convolution_convert_fusion = bf16[2048,2560]{1,0:T(8,128)(2,1)} fusion(bf16[512,2048]{1,0:T(8,128)(2,1)} %get-tuple-element.40, bf16[512,2560]{1,0:T(8,128)(2,1)S(1)} %copy-done.39), kind=kOutput, calls=%fused_computation | convolution fusion | flops 5373952000 | bytes 15204352 | tf_op jit(solution)/shard_map/dot_general | solution.py:52
  503.1 13.2 %collective-permute-done.26 = bf16[128,2048]{1,0:T(8,128)(2,1)S(1)} collective-permute-done((bf16[128,2048]{1,0:T(8,128)(2,1)}, bf16[128,2048]{1,0:T(8,128)(2,1)S(1)}, u32[]{:S(2)}, u32[]{:S(2)}) %collective-permute-start.26) | collective-permute-done | bytes 524320 | tf_op jit(solution)/shard_map/ppermute | solution.py:79
  533.0 12.1 %collective-permute-done.28 = bf16[128,2048]{1,0:T(8,128)(2,1)} collective-permute-done((bf16[128,2048]{1,0:T(8,128)(2,1)}, bf16[128,2048]{1,0:T(8,128)(2,1)}, u32[]{:S(2)}, u32[]{:S(2)}) %collective-permute-start.28) | collective-permute-done | bytes 524320 | tf_op jit(solution)/shard_map/ppermute | solution.py:84
  556.3 9.6 %collective-permute-start.18 = (bf16[128,2048]{1,0:T(8,128)(2,1)}, bf16[128,2048]{1,0:T(8,128)(2,1)}, u32[]{:S(2)}, u32[]{:S(2)}) collective-permute-start(bf16[128,2048]{1,0:T(8,128)(2,1)} %get-tuple-element.80), channel_id=1, source_target_pairs={{0,3},{1,0},{2,1},{3,2},{4,7},{5,4},{6,5},{7,6},{8,11},{9,8},{10,9... | collective-permute-start | bytes 1572872 | tf_op jit(solution)/shard_map/ppermute | solution.py:83
  568.1 13.8 %collective-permute-done.32 = f32[2,2,64]{2,1,0:T(2,128)S(1)} collective-permute-done((f32[2,2,64]{2,1,0:T(2,128)S(1)}, f32[2,2,64]{2,1,0:T(2,128)S(1)}, u32[]{:S(2)}, u32[]{:S(2)}) %collective-permute-start.32) | collective-permute-done | bytes 1056 | tf_op jit(solution)/shard_map/ppermute | solution.py:126
  593.0 49.3 %reduce-scatter.9.cloned.1.call-done = bf16[256,2560]{1,0:T(8,128)(2,1)} async-done(((bf16[2048,2560]{1,0:T(8,128)(2,1)}), bf16[256,2560]{1,0:T(8,128)(2,1)}) %reduce-scatter.9.cloned.1.call-update) | async-done | bytes 1310736 | tf_op jit(solution)/shard_map/reduce_scatter | solution.py:914
  (257 shorter events, 213.8 us)
Async XLA Ops:
  7.2 55.0 %all-gather.5.cloned.1.call-start = ((), (), s32[]{:S(2)}) async-start(), calls=%async_computation.8 | async-start | bytes 7077888 | tf_op jit(solution)/shard_map/all_gather | solution.py:857
  9.4 138.2 %all-gather.7.cloned.1.call-start = ((), (), s32[]{:S(2)}) async-start(), calls=%async_computation.9 | async-start | bytes 2359296 | tf_op jit(solution)/shard_map/all_gather | solution.py:860
  10.2 250.7 %all-gather.11.cloned.1.call-start = ((), (), s32[]{:S(2)}) async-start(), calls=%async_computation.11 | async-start | bytes 5898240 | tf_op jit(solution)/shard_map/all_gather | solution.py:862
  10.9 258.2 %all-gather.9.cloned.1.call-start = ((), (), s32[]{:S(2)}) async-start(), calls=%async_computation.10 | async-start | bytes 11796480 | tf_op jit(solution)/shard_map/all_gather | solution.py:861
  14.7 32.3 %collective-permute-start.1 = (bf16[128,2048]{1,0:T(8,128)(2,1)S(1)}, bf16[128,2048]{1,0:T(8,128)(2,1)S(1)}, u32[]{:S(2)}, u32[]{:S(2)}) collective-permute-start(bf16[128,2048]{1,0:T(8,128)(2,1)S(1)} %copy-done.1), channel_id=1, source_target_pairs={{0,3},{1,0},{2,1},{3,2},{4,7},{5,4},{6,5},{7,6},{8,11},{9,8},{10,9... | collective-permute-start | bytes 1572872 | tf_op jit(solution)/shard_map/ppermute | solution.py:65
  19.8 27.2 %collective-permute-start = (bf16[128,2048]{1,0:T(8,128)(2,1)S(1)}, bf16[128,2048]{1,0:T(8,128)(2,1)S(1)}, u32[]{:S(2)}, u32[]{:S(2)}) collective-permute-start(bf16[128,2048]{1,0:T(8,128)(2,1)S(1)} %copy-done.1), channel_id=1, source_target_pairs={{0,1},{1,2},{2,3},{3,0},{4,5},{5,6},{6,7},{7,4},{8,9},{9,10},{10,1... | collective-permute-start | bytes 1572872 | tf_op jit(solution)/shard_map/ppermute | solution.py:64
  20.0 22.3 %collective-permute-start.3 = (f32[1,1,160]{2,0,1:T(1,128)S(1)}, f32[1,1,160]{2,0,1:T(1,128)S(1)}, u32[]{:S(2)}, u32[]{:S(2)}) collective-permute-start(f32[1,1,160]{2,0,1:T(1,128)S(1)} %bitcast.83), channel_id=1, source_target_pairs={{0,1},{1,0},{2,3},{3,2},{4,5},{5,4},{6,7},{7,6},{8,9},{9,8},{10,11... | collective-permute-start | bytes 1928 | tf_op jit(solution)/shard_map/ppermute | solution.py:104
  72.5 30.5 %all-to-all-start = ((bf16[8,768,128]{2,1,0:T(8,128)(2,1)}), bf16[8,768,128]{2,1,0:T(8,128)(2,1)S(1)}, u32[]{:S(2)}, u32[]{:S(2)}) async-start(bf16[8,768,128]{2,1,0:T(8,128)(2,1)} %copy-done.9), calls=%async_computation | async-start | bytes 3145728 | tf_op jit(solution)/shard_map/all_to_all | solution.py:886
  147.5 439.1 %reduce-scatter.7.cloned.1.call-start = ((), (), s32[]{:S(2)}) async-start(), calls=%async_computation.13 | async-start | bytes 2359296 | tf_op jit(solution)/shard_map/reduce_scatter | solution.py:925
  175.8 26.2 %collective-permute-start.9 = (bf16[128,2048]{1,0:T(8,128)(2,1)}, bf16[128,2048]{1,0:T(8,128)(2,1)}, u32[]{:S(2)}, u32[]{:S(2)}) collective-permute-start(bf16[128,2048]{1,0:T(8,128)(2,1)} %get-tuple-element.82), channel_id=1, source_target_pairs={{0,3},{1,0},{2,1},{3,2},{4,7},{5,4},{6,5},{7,6},{8,11},{9,8},{10,9... | collective-permute-start | bytes 1572872 | tf_op jit(solution)/shard_map/ppermute | solution.py:83
  178.0 24.4 %collective-permute-start.10 = (bf16[128,2048]{1,0:T(8,128)(2,1)}, bf16[128,2048]{1,0:T(8,128)(2,1)}, u32[]{:S(2)}, u32[]{:S(2)}) collective-permute-start(bf16[128,2048]{1,0:T(8,128)(2,1)} %get-tuple-element.83), channel_id=1, source_target_pairs={{0,1},{1,2},{2,3},{3,0},{4,5},{5,6},{6,7},{7,4},{8,9},{9,10},{10,1... | collective-permute-start | bytes 1572872 | tf_op jit(solution)/shard_map/ppermute | solution.py:84
  178.0 46.4 %collective-permute-start.15 = (bf16[128,2048]{1,0:T(8,128)(2,1)S(1)}, bf16[128,2048]{1,0:T(8,128)(2,1)}, u32[]{:S(2)}, u32[]{:S(2)}) collective-permute-start(bf16[128,2048]{1,0:T(8,128)(2,1)S(1)} %copy-done.22), channel_id=1, source_target_pairs={{0,3},{1,0},{2,1},{3,2},{4,7},{5,4},{6,5},{7,6},{8,11},{9,8},{10,9... | collective-permute-start | bytes 1572872 | tf_op jit(solution)/shard_map/ppermute | solution.py:65
  181.8 43.1 %collective-permute-start.14 = (bf16[128,2048]{1,0:T(8,128)(2,1)S(1)}, bf16[128,2048]{1,0:T(8,128)(2,1)}, u32[]{:S(2)}, u32[]{:S(2)}) collective-permute-start(bf16[128,2048]{1,0:T(8,128)(2,1)S(1)} %copy-done.22), channel_id=1, source_target_pairs={{0,1},{1,2},{2,3},{3,0},{4,5},{5,6},{6,7},{7,4},{8,9},{9,10},{10,1... | collective-permute-start | bytes 1572872 | tf_op jit(solution)/shard_map/ppermute | solution.py:64
  204.5 42.1 %collective-permute-start.12 = (bf16[128,2048]{1,0:T(8,128)(2,1)S(1)}, bf16[128,2048]{1,0:T(8,128)(2,1)S(1)}, u32[]{:S(2)}, u32[]{:S(2)}) collective-permute-start(bf16[128,2048]{1,0:T(8,128)(2,1)S(1)} %multiply_convert_fusion.refs_0_), channel_id=1, source_target_pairs={{0,3},{1,0},{2,1},{3,2},{4,7},{5,4},{6,5},{7,6},{8,11},{9,8},{10,9... | collective-permute-start | bytes 1572872 | tf_op jit(solution)/shard_map/ppermute | solution.py:65
  211.8 35.6 %collective-permute-start.11 = (bf16[128,2048]{1,0:T(8,128)(2,1)S(1)}, bf16[128,2048]{1,0:T(8,128)(2,1)S(1)}, u32[]{:S(2)}, u32[]{:S(2)}) collective-permute-start(bf16[128,2048]{1,0:T(8,128)(2,1)S(1)} %multiply_convert_fusion.refs_0_), channel_id=1, source_target_pairs={{0,1},{1,2},{2,3},{3,0},{4,5},{5,6},{6,7},{7,4},{8,9},{9,10},{10,1... | collective-permute-start | bytes 1572872 | tf_op jit(solution)/shard_map/ppermute | solution.py:64
  225.0 35.9 %collective-permute-start.16 = (bf16[128,2048]{1,0:T(8,128)(2,1)S(1)}, bf16[128,2048]{1,0:T(8,128)(2,1)}, u32[]{:S(2)}, u32[]{:S(2)}) collective-permute-start(bf16[128,2048]{1,0:T(8,128)(2,1)S(1)} %select_select_fusion.1), channel_id=1, source_target_pairs={{1,0},{3,1},{0,2},{2,3},{5,4},{7,5},{4,6},{6,7},{9,8},{11,9},{8,10... | collective-permute-start | bytes 1572872 | tf_op jit(solution)/shard_map/ppermute | solution.py:67
  247.8 21.4 %collective-permute-start.13 = (bf16[128,2048]{1,0:T(8,128)(2,1)S(1)}, bf16[128,2048]{1,0:T(8,128)(2,1)}, u32[]{:S(2)}, u32[]{:S(2)}) collective-permute-start(bf16[128,2048]{1,0:T(8,128)(2,1)S(1)} %select_select_fusion.2), channel_id=1, source_target_pairs={{1,0},{3,1},{0,2},{2,3},{5,4},{7,5},{4,6},{6,7},{9,8},{11,9},{8,10... | collective-permute-start | bytes 1572872 | tf_op jit(solution)/shard_map/ppermute | solution.py:67
  315.6 24.0 %collective-permute-start.22 = (bf16[128,2048]{1,0:T(8,128)(2,1)S(1)}, bf16[128,2048]{1,0:T(8,128)(2,1)S(1)}, u32[]{:S(2)}, u32[]{:S(2)}) collective-permute-start(bf16[128,2048]{1,0:T(8,128)(2,1)S(1)} %get-tuple-element.79), channel_id=1, source_target_pairs={{0,1},{1,2},{2,3},{3,0},{4,5},{5,6},{6,7},{7,4},{8,9},{9,10},{10,1... | collective-permute-start | bytes 1572872 | tf_op jit(solution)/shard_map/ppermute | solution.py:84
  374.7 213.7 %reduce-scatter.11.cloned.1.call-start = ((), (), s32[]{:S(2)}) async-start(), calls=%async_computation.15 | async-start | bytes 5898240 | tf_op jit(solution)/shard_map/reduce_scatter | solution.py:917
  382.3 208.4 %reduce-scatter.5.cloned.1.call-start = ((), (), s32[]{:S(2)}) async-start(), calls=%async_computation.12 | async-start | bytes 7077888 | tf_op jit(solution)/shard_map/reduce_scatter | solution.py:939
  487.4 154.9 %reduce-scatter.9.cloned.1.call-start = ((), (), s32[]{:S(2)}) async-start(), calls=%async_computation.14 | async-start | bytes 11796480 | tf_op jit(solution)/shard_map/reduce_scatter | solution.py:914
  520.4 24.8 %collective-permute-start.28 = (bf16[128,2048]{1,0:T(8,128)(2,1)}, bf16[128,2048]{1,0:T(8,128)(2,1)}, u32[]{:S(2)}, u32[]{:S(2)}) collective-permute-start(bf16[128,2048]{1,0:T(8,128)(2,1)} %get-tuple-element.77), channel_id=1, source_target_pairs={{0,1},{1,2},{2,3},{3,0},{4,5},{5,6},{6,7},{7,4},{8,9},{9,10},{10,1... | collective-permute-start | bytes 1572872 | tf_op jit(solution)/shard_map/ppermute | solution.py:84
  528.9 24.8 %collective-permute-start.17 = (bf16[128,2048]{1,0:T(8,128)(2,1)}, bf16[128,2048]{1,0:T(8,128)(2,1)}, u32[]{:S(2)}, u32[]{:S(2)}) collective-permute-start(bf16[128,2048]{1,0:T(8,128)(2,1)} %slice.205), channel_id=1, source_target_pairs={{0,1},{1,3},{2,0},{3,2},{4,5},{5,7},{6,4},{7,6},{8,9},{9,11},{10,8... | collective-permute-start | bytes 1572872 | tf_op jit(solution)/shard_map/ppermute | solution.py:79
  556.3 25.6 %collective-permute-start.18 = (bf16[128,2048]{1,0:T(8,128)(2,1)}, bf16[128,2048]{1,0:T(8,128)(2,1)}, u32[]{:S(2)}, u32[]{:S(2)}) collective-permute-start(bf16[128,2048]{1,0:T(8,128)(2,1)} %get-tuple-element.80), channel_id=1, source_target_pairs={{0,3},{1,0},{2,1},{3,2},{4,7},{5,4},{6,5},{7,6},{8,11},{9,8},{10,9... | collective-permute-start | bytes 1572872 | tf_op jit(solution)/shard_map/ppermute | solution.py:83
  (62 other events, 937.0 us)
Sparse Core Ops, SparseCore 0:
  10.5 48.5 all-gather.4
  61.0 38.1 all-gather.6
  101.0 43.6 all-gather.10
  147.0 63.1 all-gather.8
  374.9 40.0 reduce-scatter.6
  418.6 72.9 reduce-scatter.10
  495.0 61.8 reduce-scatter.4
  560.8 81.4 reduce-scatter.8

commit v2 on v1

--- a/solution.py
+++ b/solution.py
@@ -56,34 +56,57 @@
     return [(i, (i + by) % count) for i in range(count)]
 
 
-def gather_slots(rows):
+def together(*values):
+    return lax.optimization_barrier(values)
+
+
+def gather_near(rows):
     count = lax.axis_size("head")
     if count != 4:
         return [rows] + [lax.ppermute(rows, "head", cyclic(count, s)) for s in range(1, count)]
+    return [rows, lax.ppermute(rows, "head", cyclic(4, 1)), lax.ppermute(rows, "head", cyclic(4, 3))]
+
+
+def gather_far(near):
+    if lax.axis_size("head") != 4:
+        return near
+    rows, back_one, ahead_one = near
     me = lax.axis_index("head")
-    back_one = lax.ppermute(rows, "head", cyclic(4, 1))
-    ahead_one = lax.ppermute(rows, "head", cyclic(4, 3))
     passed = jnp.where(me == 1, ahead_one, jnp.where(me == 2, back_one, rows))
     back_two = lax.ppermute(passed, "head", [(1, 0), (3, 1), (0, 2), (2, 3)])
     return [rows, back_one, back_two, ahead_one]
 
 
-def sum_slots(parts):
+def sum_far(parts):
     count = lax.axis_size("head")
     if count != 4:
-        total = parts[0].astype(f32)
-        for s in range(1, count):
-            total = total + lax.ppermute(parts[s], "head", cyclic(count, count - s)).astype(f32)
+        return []
+    return [lax.ppermute(parts[2], "head", [(0, 1), (1, 3), (2, 0), (3, 2)])]
+
+
+def sum_near(parts, far):
+    count = lax.axis_size("head")
+    if count != 4:
+        return [parts[0]] + [
+            lax.ppermute(parts[s], "head", cyclic(count, count - s)) for s in range(1, count)
+        ]
+    me = lax.axis_index("head")
+    wide = far[0].astype(f32)
+    to_back = jnp.where(me == 2, parts[1].astype(f32) + wide, parts[1].astype(f32)).astype(bf16)
+    to_ahead = jnp.where(me == 1, parts[3].astype(f32) + wide, parts[3].astype(f32)).astype(bf16)
+    from_ahead = lax.ppermute(to_back, "head", cyclic(4, 3))
+    from_back = lax.ppermute(to_ahead, "head", cyclic(4, 1))
+    return [parts[0], from_ahead, from_back, far[0]]
+
+
+def sum_terms(terms):
+    total = terms[0].astype(f32) + terms[1].astype(f32) + terms[2].astype(f32)
+    if lax.axis_size("head") != 4:
+        for term in terms[3:]:
+            total = total + term.astype(f32)
         return total
     me = lax.axis_index("head")
-    far = lax.ppermute(parts[2], "head", [(0, 1), (1, 3), (2, 0), (3, 2)])
-    far_wide = far.astype(f32)
-    to_back = jnp.where(me == 2, parts[1].astype(f32) + far_wide, parts[1].astype(f32)).astype(bf16)
-    to_ahead = jnp.where(me == 1, parts[3].astype(f32) + far_wide, parts[3].astype(f32)).astype(bf16)
-    from_ahead = lax.ppermute(to_back, "head", cyclic(4, 3))
-    from_back = lax.ppermute(to_ahead, "head", cyclic(4, 1))
-    mine = parts[0].astype(f32) + from_ahead.astype(f32) + from_back.astype(f32)
-    return mine + jnp.where((me == 0) | (me == 3), far_wide, 0.0)
+    return total + jnp.where((me == 0) | (me == 3), terms[3].astype(f32), 0.0)
 
 
 def is_power(count):
@@ -111,22 +134,17 @@
     return held
 
 
-def scatter_small(values):
-    for axis in ("blk", "head"):
-        count = lax.axis_size(axis)
-        if not is_power(count):
-            values = lax.psum_scatter(values, axis, scatter_dimension=0, tiled=False)
-            continue
-        me = lax.axis_index(axis)
-        bit = count // 2
-        while bit >= 1:
-            upper = (me // bit) % 2 == 1
-            low, high = values[:bit], values[bit:]
-            kept, sent = jnp.where(upper, high, low), jnp.where(upper, low, high)
-            values = kept + lax.ppermute(sent, axis, [(i, i ^ bit) for i in range(count)])
-            bit //= 2
-        values = values[0]
-    return values
+def scatter_blk(values):
+    return jnp.sum(lax.all_to_all(values, "blk", 0, 0, tiled=True), axis=0)
+
+
+def scatter_head(values):
+    count, me = lax.axis_size("head"), lax.axis_index("head")
+    total = lax.dynamic_index_in_dim(values, me, 0, False)
+    for s in range(1, count):
+        sent = lax.dynamic_index_in_dim(values, (me + s) % count, 0, False)
+        total = total + lax.ppermute(sent, "head", cyclic(count, s))
+    return total
 
 
 def lane_low(shape):
@@ -147,15 +165,17 @@
 
 def project_kernel(slots, *refs):
     x_refs = refs[:slots]
-    gain_ref, wq_ref, wk_ref, wv_ref, normed_ref, packed_ref = refs[slots:]
+    gain_ref, wq_ref, wk_ref, wv_ref, normed_ref, packed_ref, scale_ref = refs[slots:]
     rows = slots * SPAN
 
     @pl.when(pl.program_id(0) == 0)
     def _():
         for s in range(slots):
             wide = x_refs[s][...].astype(f32)
-            normed = wide * rms_scale(wide) * gain_ref[...]
+            scale = rms_scale(wide)
+            normed = wide * scale * gain_ref[...]
             normed_ref[s * SPAN : (s + 1) * SPAN, :] = normed.astype(bf16)
+            scale_ref[s * SPAN : (s + 1) * SPAN, :] = jnp.broadcast_to(scale, (SPAN, LANES))
 
     normed = normed_ref[...]
     query = dot_nn(normed, wq_ref[...])
@@ -191,10 +211,12 @@
         out_specs=[
             pl.BlockSpec((rows, depth), lambda j: (0, 0)),
             pl.BlockSpec((tile // HD, rows + rows // 2, LANES), lambda j: (j, 0, 0)),
+            pl.BlockSpec((rows, LANES), lambda j: (0, 0)),
         ],
         out_shape=[
             jax.ShapeDtypeStruct((rows, depth), bf16),
             jax.ShapeDtypeStruct((heads, rows + rows // 2, LANES), bf16),
+            jax.ShapeDtypeStruct((rows, LANES), f32),
         ],
         compiler_params=pltpu.CompilerParams(vmem_limit_bytes=40 * MIB),
         cost_estimate=pl.CostEstimate(
@@ -631,7 +653,7 @@
 
 def feed_kernel(slots, *refs):
     normed_refs, grad_refs = refs[:slots], refs[slots : 2 * slots]
-    both_ref, down_ref, rows_ref, rows_grad_ref, active_ref, d_both_ref = refs[2 * slots :]
+    gate_ref, up_ref, down_ref, rows_ref, rows_grad_ref, active_ref, d_both_ref = refs[2 * slots :]
 
     @pl.when(pl.program_id(0) == 0)
     def _():
@@ -640,9 +662,10 @@
             rows_grad_ref[s * SPAN : (s + 1) * SPAN, :] = grad_refs[s][...]
 
     tile = down_ref.shape[0]
-    pre = dot_nn(rows_ref[...], both_ref[...])
+    width = d_both_ref.shape[1] // 2
+    gate = dot_nn(rows_ref[...], gate_ref[...])
+    up = dot_nn(rows_ref[...], up_ref[...])
     d_hidden = dot_nt(rows_grad_ref[...], down_ref[...])
-    gate, up = pre[:, :tile], pre[:, tile:]
     scale, cubic = 0.7978845608028654, 0.044715
     square = gate * gate
     bent = jnp.tanh(scale * (gate + cubic * square * gate))
@@ -650,8 +673,9 @@
     gelu = gate * half
     slope = half + 0.5 * gate * (1.0 - bent * bent) * (scale * (1.0 + 3.0 * cubic * square))
     active_ref[...] = (gelu * up).astype(bf16)
-    d_both_ref[:, :tile] = (d_hidden * up * slope).astype(bf16)
-    d_both_ref[:, tile:] = (d_hidden * gelu).astype(bf16)
+    start = pl.program_id(0) * tile
+    d_both_ref[:, dyn(start, tile, tile)] = (d_hidden * up * slope).astype(bf16)
+    d_both_ref[:, dyn(width + start, tile, LANES)] = (d_hidden * gelu).astype(bf16)
 
 
 def feed_tile(width):
@@ -662,21 +686,23 @@
     slots = len(normed_slots)
     rows, depth, width = slots * SPAN, both.shape[0], down.shape[0]
     tile = feed_tile(width)
+    steps = width // tile
     whole = pl.BlockSpec((SPAN, depth), lambda j: (0, 0))
     rows_spec = pl.BlockSpec((rows, depth), lambda j: (0, 0))
     return pl.pallas_call(
         functools.partial(feed_kernel, slots),
-        grid=(width // tile,),
+        grid=(steps,),
         in_specs=[whole] * (2 * slots)
         + [
-            pl.BlockSpec((depth, 2 * tile), lambda j: (0, j)),
+            pl.BlockSpec((depth, tile), lambda j: (0, j)),
+            pl.BlockSpec((depth, tile), lambda j: (0, steps + j)),
             pl.BlockSpec((tile, depth), lambda j: (j, 0)),
         ],
         out_specs=[
             rows_spec,
             rows_spec,
             pl.BlockSpec((rows, tile), lambda j: (0, j)),
-            pl.BlockSpec((rows, 2 * tile), lambda j: (0, j)),
+            pl.BlockSpec((rows, 2 * width), lambda j: (0, 0)),
         ],
         out_shape=[
             jax.ShapeDtypeStruct((rows, depth), bf16),
@@ -691,7 +717,7 @@
             transcendentals=rows * width,
         ),
         name="feed",
-    )(*normed_slots, *grad_slots, both, down)
+    )(*normed_slots, *grad_slots, both, both, down)
 
 
 def mix_back_kernel(slots, *refs):
@@ -738,7 +764,9 @@
     )(*grad_slots, weight)
 
 
-def project_back_kernel(slots, packed_ref, weight_ref, grads_ref, part_ref):
+def project_back_kernel(slots, packed_ref, weight_ref, scale_ref, *refs):
+    x_refs = refs[:slots]
+    grads_ref, part_ref, gain_ref = refs[slots:]
     heads = packed_ref.shape[0]
     rows = slots * SPAN
     half = rows // 2
@@ -756,12 +784,18 @@
             grads_ref[:, width + start : width + start + LANES] = key.astype(bf16)
             grads_ref[:, 2 * width + start : 2 * width + start + LANES] = value.astype(bf16)
 
-    part = dot_nt(grads_ref[...], weight_ref[...]).astype(bf16)
+    part = dot_nt(grads_ref[...], weight_ref[...])
+    gain = jnp.zeros((1, part.shape[1]), f32)
     for s in range(slots):
-        part_ref[s] = part[s * SPAN : (s + 1) * SPAN]
-
-
-def project_back(packed, weights, slots):
+        span = slice(s * SPAN, (s + 1) * SPAN)
+        part_ref[s] = part[span].astype(bf16)
+        x_hat = x_refs[s][...].astype(f32) * scale_ref[span, :1]
+        gain = gain + jnp.sum(part[span] * x_hat, axis=0, keepdims=True)
+    gain_ref[...] = gain
+
+
+def project_back(packed, weights, scale, x_slots):
+    slots = len(x_slots)
     heads = packed.shape[0]
     depth, width = weights.shape
     rows = slots * SPAN
@@ -772,21 +806,25 @@
         in_specs=[
             pl.BlockSpec(packed.shape, lambda j: (0, 0, 0)),
             pl.BlockSpec((tile, width), lambda j: (j, 0)),
-        ],
+            pl.BlockSpec((rows, LANES), lambda j: (0, 0)),
+        ]
+        + [pl.BlockSpec((SPAN, tile), lambda j: (0, j))] * slots,
         out_specs=[
             pl.BlockSpec((rows, width), lambda j: (0, 0)),
             pl.BlockSpec((slots, SPAN, tile), lambda j: (0, 0, j)),
+            pl.BlockSpec((1, tile), lambda j: (0, j)),
         ],
         out_shape=[
             jax.ShapeDtypeStruct((rows, width), bf16),
             jax.ShapeDtypeStruct((slots, SPAN, depth), bf16),
+            jax.ShapeDtypeStruct((1, depth), f32),
         ],
         compiler_params=pltpu.CompilerParams(vmem_limit_bytes=40 * MIB),
         cost_estimate=pl.CostEstimate(
             flops=2 * rows * depth * width, bytes_accessed=2 * depth * width, transcendentals=0
         ),
         name="project_back",
-    )(packed, weights)
+    )(packed, weights, scale, *x_slots)
 
 
 def bucket_lines(bucket_of):
@@ -812,13 +850,6 @@
     rows.append(jnp.broadcast_to(bucket_of[-1:], (WIDE,)))
     spare = 8 * ((MID_BLOCKS + 2 + 7) // 8) - (MID_BLOCKS + 2)
     return jnp.concatenate([jnp.stack(rows), jnp.full((spare, WIDE), -1, bucket_of.dtype)])
-
-
-def interleave(first, second, tile):
-    rows = first.shape[0]
-    return jnp.concatenate(
-        [first.reshape(rows, -1, 1, tile), second.reshape(rows, -1, 1, tile)], axis=2
-    ).reshape(rows, -1)
 
 
 def on_device(
@@ -848,9 +879,9 @@
     bucket_count = table_rows * blk_count
     total = blk_count * slots * SPAN
     gain_size = gain_attn.shape[0]
-    tile = feed_tile(w_gate.shape[1])
-
-    token_slots = gather_slots(tokens)
+    hidden = w_gate.shape[1]
+
+    token_slots = gather_far(gather_near(tokens))
     small = gather_small(
         jnp.concatenate([gain_attn, gain_ffn, bias_table.astype(f32).reshape(-1)])
     )
@@ -858,7 +889,9 @@
         jnp.concatenate([w_query, w_key, w_value], axis=1), "blk", axis=0, tiled=True
     )
     full_out = lax.all_gather(w_out, "blk", axis=1, tiled=True)
-    full_both = lax.all_gather(interleave(w_gate, w_up, tile), "blk", axis=0, tiled=True)
+    full_both = lax.all_gather(
+        jnp.concatenate([w_gate, w_up], axis=1), "blk", axis=0, tiled=True
+    )
     full_down = lax.all_gather(w_down, "blk", axis=1, tiled=True)
     gain_one = small[:, :, :gain_size].reshape(1, depth)
     gain_two = small[:, :, gain_size : 2 * gain_size].reshape(1, depth)
@@ -895,62 +928,76 @@
         values = values.reshape((heads, shares) + values.shape[1:])
         return jnp.sum(values.astype(f32), axis=1).astype(bf16)
 
-    normed_one, packed = project(token_slots, gain_one, full_qkv)
-    swapped = to_heads(packed)
+    cotangent, *token_slots = together(cotangent, *token_slots)
+    normed_one, packed, scale_one = project(token_slots, gain_one, full_qkv)
+    grad_near = gather_near(cotangent)
+    swapped, *grad_near = together(to_heads(packed), *grad_near)
+    grad_slots = gather_far(grad_near)
     mixed, exact, lse = attend(block_order, ends, info, swapped, bias_rows, slots)
+    mixed, *grad_slots = together(mixed, *grad_slots)
     attn_mix, out_parts = out_project(to_rows(mixed), full_out, slots)
+    out_parts = [out_parts[s] for s in range(slots)]
     tokens_wide = tokens.astype(f32)
-    hidden_one = tokens_wide + sum_slots([out_parts[s] for s in range(slots)])
+    hidden_one = tokens_wide + sum_terms(sum_near(out_parts, sum_far(out_parts)))
     rstd_two = rms_scale(hidden_one)
     normed_two = (hidden_one * rstd_two * gain_two).astype(bf16)
 
-    grad_slots = gather_slots(cotangent)
-    normed_slots = gather_slots(normed_two)
+    normed_slots = gather_far(gather_near(normed_two))
     rows_two, rows_grad, active, d_both = feed(normed_slots, grad_slots, full_both, full_down)
-    d_parts = dot_nt(d_both, full_both).astype(bf16)
-    d_normed_two = sum_slots([d_parts[s * SPAN : (s + 1) * SPAN] for s in range(slots)])
-    down_parts = dot_nn(active, full_down).astype(bf16)
-    output = hidden_one + sum_slots([down_parts[s * SPAN : (s + 1) * SPAN] for s in range(slots)])
-    grad_both = lax.psum_scatter(
-        dot_tn(rows_two, d_both).astype(bf16), "blk", scatter_dimension=0, tiled=True
-    )
-    grad_down = lax.psum_scatter(
-        dot_tn(active, rows_grad).astype(bf16), "blk", scatter_dimension=1, tiled=True
-    )
+
+    def spans(rows):
+        return [rows[s * SPAN : (s + 1) * SPAN] for s in range(slots)]
+
+    d_parts = spans(dot_nt(d_both, full_both).astype(bf16))
+    d_far = sum_far(d_parts)
+    grad_both, *d_far = together(dot_tn(rows_two, d_both).astype(bf16), *d_far)
+    grad_both = lax.psum_scatter(grad_both, "blk", scatter_dimension=0, tiled=True)
+    d_near = sum_near(d_parts, d_far)
+    grad_down, *d_near = together(dot_tn(active, rows_grad).astype(bf16), *d_near)
+    grad_down = lax.psum_scatter(grad_down, "blk", scatter_dimension=1, tiled=True)
+    d_normed_two = sum_terms(d_near)
     d_source_two, gain_part_two = norm_back(d_normed_two, hidden_one, rstd_two, gain_two)
     d_hidden_one = cotangent.astype(f32) + d_source_two
 
-    attn_slots = gather_slots(d_hidden_one.astype(bf16))
-    rows_attn, mix_grads = mix_back(attn_slots, full_out)
+    attn_near = gather_near(d_hidden_one.astype(bf16))
+    down_parts, *attn_near = together(dot_nn(active, full_down).astype(bf16), *attn_near)
+    down_parts = spans(down_parts)
+    rows_attn, mix_grads = mix_back(gather_far(attn_near), full_out)
     grad_out = lax.psum_scatter(
         dot_tn(attn_mix, rows_attn).astype(bf16), "blk", scatter_dimension=1, tiled=True
     )
+    down_far = sum_far(down_parts)
+    mix_grads, grad_both, *down_far = together(to_heads(mix_grads), grad_both, *down_far)
+    down_near = sum_near(down_parts, down_far)
     grads = attend_back(
-        block_order, ends, info, swapped, to_heads(mix_grads), exact, lse, bias_rows, bucket_rows,
+        block_order, ends, info, swapped, mix_grads, exact, lse, bias_rows, bucket_rows,
         slots, bucket_count,
     )
+    grads, grad_down, *down_near = together(grads, grad_down, *down_near)
+    output = hidden_one + sum_terms(down_near)
     grads = swap(grads)
     extra = grads[:, -EXTRA : -EXTRA + 2, :table_rows].astype(f32).sum(axis=1)
     grad_table = extra.reshape(heads, shares, table_rows).sum(axis=1).T
     if shares > 1:
         grads = grads.reshape((heads, shares) + grads.shape[1:])
         grads = jnp.sum(grads.astype(f32), axis=1).astype(bf16)
-    d_qkv, d_parts_one = project_back(grads, full_qkv, slots)
-    grad_qkv = lax.psum_scatter(
-        dot_tn(normed_one, d_qkv).astype(bf16), "blk", scatter_dimension=0, tiled=True
-    )
-    d_normed_one = sum_slots([d_parts_one[s] for s in range(slots)])
-    d_source_one, gain_part_one = norm_back(
-        d_normed_one, tokens_wide, rms_scale(tokens_wide), gain_one
-    )
-    input_grad = d_hidden_one + d_source_one
+    d_qkv, one_parts, gain_part_one = project_back(grads, full_qkv, scale_one, token_slots)
+    one_parts = [one_parts[s] for s in range(slots)]
+    one_far = sum_far(one_parts)
     gain_parts = jnp.stack(
         [part.reshape(blk_count, slots, gain_size) for part in (gain_part_one, gain_part_two)],
         axis=2,
     )
-    gain_sums = scatter_small(gain_parts)
-    grad_qkv = grad_qkv.astype(f32)
-    grad_both = grad_both.astype(f32).reshape(grad_both.shape[0], -1, 2, tile)
+    grad_qkv, gain_parts = together(dot_tn(normed_one, d_qkv).astype(bf16), gain_parts)
+    grad_qkv, gain_sums, grad_out, *one_far = together(
+        grad_qkv, scatter_blk(gain_parts), grad_out, *one_far
+    )
+    grad_qkv = lax.psum_scatter(grad_qkv, "blk", scatter_dimension=0, tiled=True).astype(f32)
+    gain_sums, *one_near = together(scatter_head(gain_sums), *sum_near(one_parts, one_far))
+    d_normed_one = sum_terms(one_near)
+    d_source_one, unused = norm_back(d_normed_one, tokens_wide, rms_scale(tokens_wide), gain_one)
+    input_grad = d_hidden_one + d_source_one
+    grad_both = grad_both.astype(f32)
     return (
         output,
         input_grad,
@@ -961,8 +1008,8 @@
         grad_out.astype(f32),
         grad_table,
         gain_sums[1],
-        grad_both[:, :, 0].reshape(w_gate.shape),
-        grad_both[:, :, 1].reshape(w_up.shape),
+        grad_both[:, :hidden],
+        grad_both[:, hidden:],
         grad_down.astype(f32),
     )
 

time: 672 us -> 567 us (0.84)
  waiting for transfers between devices: 296 us -> 235 us
  blocking collectives: 48.7 us -> 7.35 us
    ppermute x29 -> x27, waiting for transfers between devices: 186 us -> 134 us  [the longest x4 27.4 us: gather_near(): lax.ppermute(rows, 'head', cyclic(4, 1))]
    all_to_all x2 -> x1, blocking collectives: 48.7 us -> 7.35 us  [scatter_blk(): return jnp.sum(lax.all_to_all(values, 'blk', 0, 0, tiled=True), axis=0)]
    reduce_scatter x3, waiting for transfers between devices: 49.3 us -> 24.3 us  [the longest x1 24.3 us: on_device(): lax.psum_scatter(grad_qkv, 'blk', scatter_dimension=0, tiled=True)]
    ppermute x29 -> x27, starting transfers between devices: 68.8 us -> 45.7 us  [the longest x4 11.5 us: gather_near(): lax.ppermute(rows, 'head', cyclic(4, 3))]
    all_to_all x2 -> x4, starting transfers between devices: 7.36 us -> 24.6 us  [swap(): return lax.all_to_all(values, 'blk', 0, 0, tiled=True)]
    all_to_all x2 -> x4, waiting for transfers between devices: 29.1 us -> 43.9 us  [swap(): return lax.all_to_all(values, 'blk', 0, 0, tiled=True)]
    unnamed x94 -> x132, local copies, waits for them, and re-layouts: 22.5 us -> 32.2 us
  transfers between devices with their start and end apart: 44 -> 44, of which waited for: 28 -> 24; matrix products, arithmetic and copies ran while one was open for 10% -> 12% of each run, Pallas kernels for 14% -> 17%
where the time goes in v2:
time: 567 us; the launch traced here: 558 us
  waiting for transfers between devices  235 us (41%)
  Pallas kernels  112 us (20%)
  starting transfers between devices  75 us (13%)
  local copies, waits for them, and re-layouts  45.2 us (8%)
  matrix products  38.8 us (7%)
  other arithmetic  29.6 us (5%)
  between operations  15.4 us (3%)
  blocking collectives  7.35 us (1%)
    all_to_all x4, waiting for transfers between devices, swap(): return lax.all_to_all(values, 'blk', 0, 0, tiled=True)  43.9 us
    pallas_call x1, Pallas kernels, attend_back(): pl.pallas_call(functools.partial(attend_back_kernel, slots, bucket_count)...  41.8 us
    pallas_call x1, Pallas kernels, attend(): pl.pallas_call(functools.partial(attend_kernel, slots), in_specs=[smem_sp...  40.2 us
    unnamed x132, local copies, waits for them, and re-layouts  32.2 us
    ppermute x5, waiting for transfers between devices, gather_small(): other = lax.ppermute(held, axis, [(i, i ^ bit) for i in range(count)])  30.5 us
    ppermute x4, waiting for transfers between devices, gather_near(): lax.ppermute(rows, 'head', cyclic(4, 1))  27.4 us
    ppermute x4, waiting for transfers between devices, gather_far(): back_two = lax.ppermute(passed, 'head', [(1, 0), (3, 1), (0, 2), (2, 3)])  25.5 us
    all_to_all x4, starting transfers between devices, swap(): return lax.all_to_all(values, 'blk', 0, 0, tiled=True)  24.6 us
  transfers between devices with their start and end apart: 44, of which 24 were waited for; matrix products, arithmetic and copies ran while one was open for 12% of the time, Pallas kernels for 17%

profile of v2, /device:TPU:0, one launch (start us, length us, event | category | flops | bytes accessed | tf_op | source)
XLA Modules:
  0.0 557.8 jit_solution(10286912298252166205)
XLA Ops:
  17.6 22.4 %collective-permute-done.3 = f32[1,1,160]{2,0,1:T(1,128)S(1)} collective-permute-done((f32[1,1,160]{2,0,1:T(1,128)S(1)}, f32[1,1,160]{2,0,1:T(1,128)S(1)}, u32[]{:S(2)}, u32[]{:S(2)}) %collective-permute-start.3) | collective-permute-done | bytes 672 | tf_op jit(solution)/shard_map/ppermute | solution.py:127
  84.0 7.4 %collective-permute-done.8.refs_5_ = bf16[128,2048]{1,0:T(8,128)(2,1)} collective-permute-done((bf16[128,2048]{1,0:T(8,128)(2,1)S(1)}, bf16[128,2048]{1,0:T(8,128)(2,1)}, u32[]{:S(2)}, u32[]{:S(2)}) %collective-permute-start.8) | collective-permute-done | bytes 524320 | tf_op jit(solution)/shard_map/ppermute | solution.py:67
  91.4 9.9 %collective-permute-done.9.refs_7_ = bf16[128,2048]{1,0:T(8,128)(2,1)} collective-permute-done((bf16[128,2048]{1,0:T(8,128)(2,1)S(1)}, bf16[128,2048]{1,0:T(8,128)(2,1)}, u32[]{:S(2)}, u32[]{:S(2)}) %collective-permute-start.9) | collective-permute-done | bytes 524320 | tf_op jit(solution)/shard_map/ppermute | solution.py:67
  105.6 40.2 %attend.1 = (bf16[8,256,128]{2,1,0:T(8,128)(2,1)}, f32[64,4096]{1,0:T(8,128)S(1)}, f32[1,4096]{1,0:T(1,128)S(1)}) custom-call(s32[32]{0:T(128)S(1)} %copy-done.21, s32[2]{0:T(128)S(1)} %bitcast.67, s32[3]{0:T(128)S(1)} %pad_add_fusion.2.info_ref, bf16[8,768,128]{2,1,0:T(8,128)(2,1)S(1)} %all-to-all-done.x_ref, f32[8,512]{1,0:T(8,128)S(1)} %select_reduce_fusion.bias_ref), custom_call_target="tpu_custom_call" | custom-call | flops 2147483648 | bytes 8388608 | tf_op jit(solution)/shard_map/attend/pallas_call | solution.py:411
  150.8 13.0 %all-to-all-done.1.packed_ref = bf16[8,256,128]{2,1,0:T(8,128)(2,1)S(1)} async-done(((bf16[8,256,128]{2,1,0:T(8,128)(2,1)}), bf16[8,256,128]{2,1,0:T(8,128)(2,1)S(1)}, u32[]{:S(2)}, u32[]{:S(2)}) %all-to-all-start.1) | async-done | bytes 524320 | tf_op jit(solution)/shard_map/all_to_all | solution.py:919
  170.4 11.3 %collective-permute-done.11 = bf16[128,2048]{1,0:T(8,128)(2,1)S(1)} collective-permute-done((bf16[128,2048]{1,0:T(8,128)(2,1)S(1)}, bf16[128,2048]{1,0:T(8,128)(2,1)S(1)}, u32[]{:S(2)}, u32[]{:S(2)}) %collective-permute-start.11) | collective-permute-done | bytes 524320 | tf_op jit(solution)/shard_map/ppermute | solution.py:84
  187.7 13.0 %collective-permute-done.13 = bf16[128,2048]{1,0:T(8,128)(2,1)} collective-permute-done((bf16[128,2048]{1,0:T(8,128)(2,1)}, bf16[128,2048]{1,0:T(8,128)(2,1)}, u32[]{:S(2)}, u32[]{:S(2)}) %collective-permute-start.13) | collective-permute-done | bytes 524320 | tf_op jit(solution)/shard_map/ppermute | solution.py:98
  210.4 12.8 %collective-permute-done.14.refs_1_ = bf16[128,2048]{1,0:T(8,128)(2,1)S(1)} collective-permute-done((bf16[128,2048]{1,0:T(8,128)(2,1)S(1)}, bf16[128,2048]{1,0:T(8,128)(2,1)S(1)}, u32[]{:S(2)}, u32[]{:S(2)}) %collective-permute-start.14) | collective-permute-done | bytes 524320 | tf_op jit(solution)/shard_map/ppermute | solution.py:67
  223.3 6.6 %collective-permute-done.15.refs_3_ = bf16[128,2048]{1,0:T(8,128)(2,1)S(1)} collective-permute-done((bf16[128,2048]{1,0:T(8,128)(2,1)S(1)}, bf16[128,2048]{1,0:T(8,128)(2,1)S(1)}, u32[]{:S(2)}, u32[]{:S(2)}) %collective-permute-start.15) | collective-permute-done | bytes 524320 | tf_op jit(solution)/shard_map/ppermute | solution.py:67
  233.3 9.2 %collective-permute-done.16.refs_2_ = bf16[128,2048]{1,0:T(8,128)(2,1)} collective-permute-done((bf16[128,2048]{1,0:T(8,128)(2,1)S(1)}, bf16[128,2048]{1,0:T(8,128)(2,1)}, u32[]{:S(2)}, u32[]{:S(2)}) %collective-permute-start.16) | collective-permute-done | bytes 524320 | tf_op jit(solution)/shard_map/ppermute | solution.py:76
  242.5 14.8 %feed.1 = (bf16[512,2048]{1,0:T(8,128)(2,1)}, bf16[512,2048]{1,0:T(8,128)(2,1)}, bf16[512,1280]{1,0:T(8,128)(2,1)}, bf16[512,2560]{1,0:T(8,128)(2,1)}) custom-call(bf16[128,2048]{1,0:T(8,128)(2,1)} %copy-done.42, bf16[128,2048]{1,0:T(8,128)(2,1)} %copy-done.43, bf16[128,2048]{1,0:T(8,128)(2,1)} %collective-permute-done.16.refs_2_, ...), custom_call_target="tpu_custom_call" | custom-call | flops 8053063680 | bytes 15728640 | tf_op jit(solution)/shard_map/feed/pallas_call | solution.py:692
  257.3 9.3 %convolution_convert_fusion.5 = bf16[512,2048]{1,0:T(8,128)(2,1)S(1)} fusion(bf16[512,2560]{1,0:T(8,128)(2,1)} %get-tuple-element.93, bf16[2048,2560]{1,0:T(8,128)(2,1)} %all-gather.9.cloned.1.call-done.refs_8_.refs_9_), kind=kOutput, calls=%fused_computation.5 | convolution fusion | flops 5369757696 | bytes 15204352 | tf_op jit(solution)/shard_map/dot_general | solution.py:48
  269.0 8.4 %convolution_convert_fusion = bf16[2048,2560]{1,0:T(8,128)(2,1)} fusion(bf16[512,2048]{1,0:T(8,128)(2,1)S(1)} %copy-done.58, bf16[512,2560]{1,0:T(8,128)(2,1)S(1)} %copy-done.56), kind=kOutput, calls=%fused_computation | convolution fusion | flops 5373952000 | bytes 15204352 | tf_op jit(solution)/shard_map/dot_general | solution.py:52
  290.6 13.6 %collective-permute-done.18 = bf16[128,2048]{1,0:T(8,128)(2,1)S(1)} collective-permute-done((bf16[128,2048]{1,0:T(8,128)(2,1)}, bf16[128,2048]{1,0:T(8,128)(2,1)S(1)}, u32[]{:S(2)}, u32[]{:S(2)}) %collective-permute-start.18) | collective-permute-done | bytes 524320 | tf_op jit(solution)/shard_map/ppermute | solution.py:97
  319.4 7.1 %collective-permute-done.20.refs_1_ = bf16[128,2048]{1,0:T(8,128)(2,1)S(1)} collective-permute-done((bf16[128,2048]{1,0:T(8,128)(2,1)S(1)}, bf16[128,2048]{1,0:T(8,128)(2,1)S(1)}, u32[]{:S(2)}, u32[]{:S(2)}) %collective-permute-start.20) | collective-permute-done | bytes 524320 | tf_op jit(solution)/shard_map/ppermute | solution.py:67
  337.2 11.3 %collective-permute-done.22.refs_2_ = bf16[128,2048]{1,0:T(8,128)(2,1)S(1)} collective-permute-done((bf16[128,2048]{1,0:T(8,128)(2,1)S(1)}, bf16[128,2048]{1,0:T(8,128)(2,1)S(1)}, u32[]{:S(2)}, u32[]{:S(2)}) %collective-permute-start.22) | collective-permute-done | bytes 524320 | tf_op jit(solution)/shard_map/ppermute | solution.py:76
  352.3 13.3 %all-to-all-start.2 = ((bf16[8,256,128]{2,1,0:T(8,128)(2,1)}), bf16[8,256,128]{2,1,0:T(8,128)(2,1)S(1)}, u32[]{:S(2)}, u32[]{:S(2)}) async-start(bf16[8,256,128]{2,1,0:T(8,128)(2,1)} %get-tuple-element.103), calls=%async_computation.2 | async-start | bytes 1048576 | tf_op jit(solution)/shard_map/all_to_all | solution.py:919
  365.7 9.7 %all-to-all-done.2.mixed_ref = bf16[8,256,128]{2,1,0:T(8,128)(2,1)S(1)} async-done(((bf16[8,256,128]{2,1,0:T(8,128)(2,1)}), bf16[8,256,128]{2,1,0:T(8,128)(2,1)S(1)}, u32[]{:S(2)}, u32[]{:S(2)}) %all-to-all-start.2) | async-done | bytes 524320 | tf_op jit(solution)/shard_map/all_to_all | solution.py:919
  385.8 41.8 %attend_back.1 = bf16[8,784,128]{2,1,0:T(8,128)(2,1)S(1)} custom-call(s32[32]{0:T(128)S(1)} %copy-done.21, s32[2]{0:T(128)S(1)} %bitcast.68, s32[3]{0:T(128)S(1)} %pad_add_fusion.2.info_ref, bf16[8,768,128]{2,1,0:T(8,128)(2,1)S(1)} %copy-done.11, bf16[8,256,128]{2,1,0:T(8,128)(2,1)S(1)} %all-to-all-done.2.mixed_ref, f32[64,4096]{1,0:T(8,128)S(1)} %copy-done.26, ...), custom_call_target="tpu_custom_call" | custom-call | flops 5368709120 | bytes 12582912 | tf_op jit(solution)/shard_map/attend_back/pallas_call | solution.py:584
  432.6 21.2 %all-to-all-done.3.packed_ref = bf16[8,784,128]{2,1,0:T(8,128)(2,1)S(1)} async-done(((bf16[8,784,128]{2,1,0:T(8,128)(2,1)}), bf16[8,784,128]{2,1,0:T(8,128)(2,1)S(1)}, u32[]{:S(2)}, u32[]{:S(2)}) %all-to-all-start.3) | async-done | bytes 1605664 | tf_op jit(solution)/shard_map/all_to_all | solution.py:919
  471.8 6.8 %convolution_convert_fusion.2 = bf16[2048,1536]{1,0:T(8,128)(2,1)} fusion(bf16[512,2048]{1,0:T(8,128)(2,1)S(1)} %copy-done.18, bf16[512,1536]{1,0:T(8,128)(2,1)} %copy-done.22), kind=kOutput, calls=%fused_computation.2 | convolution fusion | flops 3224371200 | bytes 9961472 | tf_op jit(solution)/shard_map/dot_general | solution.py:52
  478.7 7.4 %all_to_all.25 = f32[8,1,512]{2,1,0:T(1,128)S(1)} all-to-all(f32[8,1,512]{2,1,0:T(1,128)S(1)} %reshape.332), channel_id=1, replica_groups=mesh['blk'=8,'head'=4] {'blk'}, dimensions={0} | all-to-all | bytes 32768 | tf_op jit(solution)/shard_map/all_to_all | solution.py:138
  502.1 13.1 %collective-permute-done.29 = f32[2,64]{1,0:T(2,128)S(1)} collective-permute-done((f32[2,64]{1,0:T(2,128)S(1)}, f32[2,64]{1,0:T(2,128)S(1)}, u32[]{:S(2)}, u32[]{:S(2)}) %collective-permute-start.29) | collective-permute-done | bytes 544 | tf_op jit(solution)/shard_map/ppermute | solution.py:146
  523.9 24.3 %reduce-scatter.11.cloned.1.call-done = bf16[256,1536]{1,0:T(8,128)(2,1)} async-done(((bf16[2048,1536]{1,0:T(8,128)(2,1)}), bf16[256,1536]{1,0:T(8,128)(2,1)}) %reduce-scatter.11.cloned.1.call-update) | async-done | bytes 786448 | tf_op jit(solution)/shard_map/reduce_scatter | solution.py:995
  (288 shorter events, 194.5 us)
Async XLA Ops:
  7.2 51.9 %all-gather.5.cloned.1.call-start = ((), (), s32[]{:S(2)}) async-start(), calls=%async_computation.9 | async-start | bytes 7077888 | tf_op jit(solution)/shard_map/all_gather | solution.py:888
  9.4 141.3 %all-gather.7.cloned.1.call-start = ((), (), s32[]{:S(2)}) async-start(), calls=%async_computation.10 | async-start | bytes 2359296 | tf_op jit(solution)/shard_map/all_gather | solution.py:891
  10.2 223.1 %all-gather.11.cloned.1.call-start = ((), (), s32[]{:S(2)}) async-start(), calls=%async_computation.12 | async-start | bytes 5898240 | tf_op jit(solution)/shard_map/all_gather | solution.py:895
  10.9 231.6 %all-gather.9.cloned.1.call-start = ((), (), s32[]{:S(2)}) async-start(), calls=%async_computation.11 | async-start | bytes 11796480 | tf_op jit(solution)/shard_map/all_gather | solution.py:892
  12.2 32.4 %collective-permute-start = (bf16[128,2048]{1,0:T(8,128)(2,1)S(1)}, bf16[128,2048]{1,0:T(8,128)(2,1)S(1)}, u32[]{:S(2)}, u32[]{:S(2)}) collective-permute-start(bf16[128,2048]{1,0:T(8,128)(2,1)S(1)} %copy-done.2), channel_id=1, source_target_pairs={{0,1},{1,2},{2,3},{3,0},{4,5},{5,6},{6,7},{7,4},{8,9},{9,10},{10,1... | collective-permute-start | bytes 1572872 | tf_op jit(solution)/shard_map/ppermute | solution.py:67
  15.3 29.4 %collective-permute-start.1 = (bf16[128,2048]{1,0:T(8,128)(2,1)S(1)}, bf16[128,2048]{1,0:T(8,128)(2,1)S(1)}, u32[]{:S(2)}, u32[]{:S(2)}) collective-permute-start(bf16[128,2048]{1,0:T(8,128)(2,1)S(1)} %copy-done.2), channel_id=1, source_target_pairs={{0,3},{1,0},{2,1},{3,2},{4,7},{5,4},{6,5},{7,6},{8,11},{9,8},{10,9... | collective-permute-start | bytes 1572872 | tf_op jit(solution)/shard_map/ppermute | solution.py:67
  17.5 22.4 %collective-permute-start.3 = (f32[1,1,160]{2,0,1:T(1,128)S(1)}, f32[1,1,160]{2,0,1:T(1,128)S(1)}, u32[]{:S(2)}, u32[]{:S(2)}) collective-permute-start(f32[1,1,160]{2,0,1:T(1,128)S(1)} %bitcast.73), channel_id=1, source_target_pairs={{0,1},{1,0},{2,3},{3,2},{4,5},{5,4},{6,7},{7,6},{8,9},{9,8},{10,11... | collective-permute-start | bytes 1928 | tf_op jit(solution)/shard_map/ppermute | solution.py:127
  69.7 31.5 %all-to-all-start = ((bf16[8,768,128]{2,1,0:T(8,128)(2,1)}), bf16[8,768,128]{2,1,0:T(8,128)(2,1)S(1)}, u32[]{:S(2)}, u32[]{:S(2)}) async-start(bf16[8,768,128]{2,1,0:T(8,128)(2,1)} %copy-done.12), calls=%async_computation | async-start | bytes 3145728 | tf_op jit(solution)/shard_map/all_to_all | solution.py:919
  75.9 25.4 %collective-permute-start.9 = (bf16[128,2048]{1,0:T(8,128)(2,1)S(1)}, bf16[128,2048]{1,0:T(8,128)(2,1)}, u32[]{:S(2)}, u32[]{:S(2)}) collective-permute-start(bf16[128,2048]{1,0:T(8,128)(2,1)S(1)} %copy-done.32), channel_id=1, source_target_pairs={{0,3},{1,0},{2,1},{3,2},{4,7},{5,4},{6,5},{7,6},{8,11},{9,8},{10,9... | collective-permute-start | bytes 1572872 | tf_op jit(solution)/shard_map/ppermute | solution.py:67
  102.3 44.5 %collective-permute-start.10 = (bf16[128,2048]{1,0:T(8,128)(2,1)}, bf16[128,2048]{1,0:T(8,128)(2,1)S(1)}, u32[]{:S(2)}, u32[]{:S(2)}) collective-permute-start(bf16[128,2048]{1,0:T(8,128)(2,1)} %select_select_fusion.2), channel_id=1, source_target_pairs={{1,0},{3,1},{0,2},{2,3},{5,4},{7,5},{4,6},{6,7},{9,8},{11,9},{8,10... | collective-permute-start | bytes 1572872 | tf_op jit(solution)/shard_map/ppermute | solution.py:76
  150.7 224.7 %reduce-scatter.5.cloned.1.call-start = ((), (), s32[]{:S(2)}) async-start(), calls=%async_computation.13 | async-start | bytes 11796480 | tf_op jit(solution)/shard_map/reduce_scatter | solution.py:954
  206.8 23.0 %collective-permute-start.15 = (bf16[128,2048]{1,0:T(8,128)(2,1)S(1)}, bf16[128,2048]{1,0:T(8,128)(2,1)S(1)}, u32[]{:S(2)}, u32[]{:S(2)}) collective-permute-start(bf16[128,2048]{1,0:T(8,128)(2,1)S(1)} %multiply_convert_fusion.refs_0_), channel_id=1, source_target_pairs={{0,3},{1,0},{2,1},{3,2},{4,7},{5,4},{6,5},{7,6},{8,11},{9,8},{10,9... | collective-permute-start | bytes 1572872 | tf_op jit(solution)/shard_map/ppermute | solution.py:67
  279.9 148.9 %reduce-scatter.7.cloned.1.call-start = ((), (), s32[]{:S(2)}) async-start(), calls=%async_computation.14 | async-start | bytes 5898240 | tf_op jit(solution)/shard_map/reduce_scatter | solution.py:957
  282.6 21.6 %collective-permute-start.18 = (bf16[128,2048]{1,0:T(8,128)(2,1)}, bf16[128,2048]{1,0:T(8,128)(2,1)S(1)}, u32[]{:S(2)}, u32[]{:S(2)}) collective-permute-start(bf16[128,2048]{1,0:T(8,128)(2,1)} %get-tuple-element.170), channel_id=1, source_target_pairs={{0,3},{1,0},{2,1},{3,2},{4,7},{5,4},{6,5},{7,6},{8,11},{9,8},{10,9... | collective-permute-start | bytes 1572872 | tf_op jit(solution)/shard_map/ppermute | solution.py:97
  310.5 22.4 %collective-permute-start.21 = (bf16[128,2048]{1,0:T(8,128)(2,1)S(1)}, bf16[128,2048]{1,0:T(8,128)(2,1)S(1)}, u32[]{:S(2)}, u32[]{:S(2)}) collective-permute-start(bf16[128,2048]{1,0:T(8,128)(2,1)S(1)} %fusion.19.refs_0_), channel_id=1, source_target_pairs={{0,3},{1,0},{2,1},{3,2},{4,7},{5,4},{6,5},{7,6},{8,11},{9,8},{10,9... | collective-permute-start | bytes 1572872 | tf_op jit(solution)/shard_map/ppermute | solution.py:67
  337.0 28.7 %collective-permute-start.23 = (bf16[128,2048]{1,0:T(8,128)(2,1)S(1)}, bf16[128,2048]{1,0:T(8,128)(2,1)S(1)}, u32[]{:S(2)}, u32[]{:S(2)}) collective-permute-start(bf16[128,2048]{1,0:T(8,128)(2,1)S(1)} %get-tuple-element.176), channel_id=1, source_target_pairs={{0,1},{1,3},{2,0},{3,2},{4,5},{5,7},{6,4},{7,6},{8,9},{9,11},{10,8... | collective-permute-start | bytes 1572872 | tf_op jit(solution)/shard_map/ppermute | solution.py:84
  352.3 23.1 %all-to-all-start.2 = ((bf16[8,256,128]{2,1,0:T(8,128)(2,1)}), bf16[8,256,128]{2,1,0:T(8,128)(2,1)S(1)}, u32[]{:S(2)}, u32[]{:S(2)}) async-start(bf16[8,256,128]{2,1,0:T(8,128)(2,1)} %get-tuple-element.103), calls=%async_computation.2 | async-start | bytes 1048576 | tf_op jit(solution)/shard_map/all_to_all | solution.py:919
  365.6 121.8 %reduce-scatter.9.cloned.1.call-start = ((), (), s32[]{:S(2)}) async-start(), calls=%async_computation.15 | async-start | bytes 2359296 | tf_op jit(solution)/shard_map/reduce_scatter | solution.py:966
  378.0 50.8 %collective-permute-start.24 = (bf16[128,2048]{1,0:T(8,128)(2,1)}, bf16[128,2048]{1,0:T(8,128)(2,1)}, u32[]{:S(2)}, u32[]{:S(2)}) collective-permute-start(bf16[128,2048]{1,0:T(8,128)(2,1)} %get-tuple-element.168), channel_id=1, source_target_pairs={{0,3},{1,0},{2,1},{3,2},{4,7},{5,4},{6,5},{7,6},{8,11},{9,8},{10,9... | collective-permute-start | bytes 1572872 | tf_op jit(solution)/shard_map/ppermute | solution.py:97
  380.2 48.7 %collective-permute-start.25 = (bf16[128,2048]{1,0:T(8,128)(2,1)}, bf16[128,2048]{1,0:T(8,128)(2,1)}, u32[]{:S(2)}, u32[]{:S(2)}) collective-permute-start(bf16[128,2048]{1,0:T(8,128)(2,1)} %get-tuple-element.167), channel_id=1, source_target_pairs={{0,1},{1,2},{2,3},{3,0},{4,5},{5,6},{6,7},{7,4},{8,9},{9,10},{10,1... | collective-permute-start | bytes 1572872 | tf_op jit(solution)/shard_map/ppermute | solution.py:98
  428.8 24.9 %all-to-all-start.3 = ((bf16[8,784,128]{2,1,0:T(8,128)(2,1)}), bf16[8,784,128]{2,1,0:T(8,128)(2,1)S(1)}, u32[]{:S(2)}, u32[]{:S(2)}) async-start(bf16[8,784,128]{2,1,0:T(8,128)(2,1)} %copy-done.9), calls=%async_computation.5 | async-start | bytes 3211264 | tf_op jit(solution)/shard_map/all_to_all | solution.py:919
  432.4 115.7 %reduce-scatter.11.cloned.1.call-start = ((), (), s32[]{:S(2)}) async-start(), calls=%async_computation.16 | async-start | bytes 7077888 | tf_op jit(solution)/shard_map/reduce_scatter | solution.py:995
  489.5 27.1 %collective-permute-start.30 = (bf16[128,2048]{1,0:T(8,128)(2,1)}, bf16[128,2048]{1,0:T(8,128)(2,1)}, u32[]{:S(2)}, u32[]{:S(2)}) collective-permute-start(bf16[128,2048]{1,0:T(8,128)(2,1)} %get-tuple-element.166), channel_id=1, source_target_pairs={{0,3},{1,0},{2,1},{3,2},{4,7},{5,4},{6,5},{7,6},{8,11},{9,8},{10,9... | collective-permute-start | bytes 1572872 | tf_op jit(solution)/shard_map/ppermute | solution.py:97
  492.5 24.1 %collective-permute-start.31 = (bf16[128,2048]{1,0:T(8,128)(2,1)}, bf16[128,2048]{1,0:T(8,128)(2,1)}, u32[]{:S(2)}, u32[]{:S(2)}) collective-permute-start(bf16[128,2048]{1,0:T(8,128)(2,1)} %get-tuple-element.165), channel_id=1, source_target_pairs={{0,1},{1,2},{2,3},{3,0},{4,5},{5,6},{6,7},{7,4},{8,9},{9,10},{10,1... | collective-permute-start | bytes 1572872 | tf_op jit(solution)/shard_map/ppermute | solution.py:98
  (82 other events, 791.9 us)
Sparse Core Ops, SparseCore 0:
  10.5 48.5 all-gather.4
  61.0 36.0 all-gather.6
  98.9 44.4 all-gather.10
  145.7 64.6 all-gather.8
  280.0 88.2 reduce-scatter.4
  371.6 56.5 reduce-scatter.6
  431.8 41.2 reduce-scatter.8
  487.6 60.5 reduce-scatter.10
